TPU v7x, 32 devices: a whole 2x2x4 slice. The times are simulated.
32 devices in a mesh: dp: 4 (over y, x), fsdp: 8 (over z, core).
Axes of the slice: x: 2, y: 2, z: 4, core: 2. Of those that a mesh axis runs over, the one named last changes fastest.
Arguments:
- tokens: bfloat16 [8192, 768], P(('dp', 'fsdp')), may hold values from -6 to 6
- memory: bfloat16 [16384, 768], P(('dp', 'fsdp')), may hold values from -6 to 6
- target_lengths: int32 [32], P(('dp', 'fsdp')), may hold values from 1 to 256, as said below
- memory_lengths: int32 [32], P(('dp', 'fsdp')), may hold values from 128 to 512, as said below
- task_ids: int32 [32], P(('dp', 'fsdp')), may hold values from 0 to 7
- cotangent: bfloat16 [8192, 768], P(('dp', 'fsdp')), may hold values from -6 to 6
- self_qkv: bfloat16 [768, 2304], P('fsdp'), may hold values from -0.21875 to 0.21875
- self_out: bfloat16 [768, 768], P('fsdp'), may hold values from -0.875 to 0.875
- cross_q: bfloat16 [768, 768], P('fsdp'), may hold values from -0.21875 to 0.21875
- cross_kv: bfloat16 [768, 1536], P('fsdp'), may hold values from -0.21875 to 0.21875
- cross_out: bfloat16 [768, 768], P('fsdp'), may hold values from -1.25 to 1.25
- ffn_in: bfloat16 [768, 3072], P('fsdp'), may hold values from -0.21875 to 0.21875
- ffn_out: bfloat16 [3072, 768], P('fsdp'), may hold values from -0.109375 to 0.109375
- task_table: float32 [8, 64], replicated, may hold values from -6 to 6
- hyper_in: float32 [64, 128], replicated, may hold values from -0.75 to 0.75
- hyper_gen: bfloat16 [128, 76032], P(None, 'fsdp'), may hold values from -0.5 to 0.5
Outputs:
- mixed_out: bfloat16 [8192, 768], P(('dp', 'fsdp'))
- token_grad: float32 [8192, 768], P(('dp', 'fsdp'))
- memory_grad: float32 [16384, 768], P(('dp', 'fsdp'))
- grad_self_qkv: float32 [768, 2304], P('fsdp')
- grad_self_out: float32 [768, 768], P('fsdp')
- grad_cross_q: float32 [768, 768], P('fsdp')
- grad_cross_kv: float32 [768, 1536], P('fsdp')
- grad_cross_out: float32 [768, 768], P('fsdp')
- grad_ffn_in: float32 [768, 3072], P('fsdp')
- grad_ffn_out: float32 [3072, 768], P('fsdp')
- grad_task_table: float32 [8, 64], replicated
- grad_hyper_in: float32 [64, 128], replicated
- grad_hyper_gen: float32 [128, 76032], P(None, 'fsdp')
Inputs may be any that keep to these rules, and one draw needn't show every extreme that they name: `target_lengths`: sequence s lies in bucket s // 8; bucket b holds lengths from b * 64 + 1 to (b + 1) * 64; some sequence of the last bucket has exactly 256. `memory_lengths`: some sequence has exactly 512.
All inputs are finite; a program needn't handle non-finite values.
Results may differ from a plain program's by a relative error of at most 0.024.
Values may be sent and summed in bfloat16 or wider, within the bound.
No kernel may reach another device: no remote copies, remote signals or barrier semaphores. Data moves between devices by JAX's collectives and lax.ppermute only.
A program may use at most 192 MiB of HBM per device.

v0:
```python
import jax
import jax.numpy as jnp
from jax import lax
from jax.sharding import PartitionSpec as P

D = 768
HEADS = 12
HEAD = 64
ADAPT = 24
TASKS = 8


def matmul(left, right):
    return jnp.dot(left, right, preferred_element_type=jnp.float32)


def matmul_left_t(left, right):
    return lax.dot_general(
        left, right, (((0,), (0,)), ((), ())), preferred_element_type=jnp.float32
    )


def matmul_right_t(left, right):
    return lax.dot_general(
        left, right, (((1,), (1,)), ((), ())), preferred_element_type=jnp.float32
    )


def rms_norm(values, gains):
    return values * lax.rsqrt(jnp.mean(values * values, axis=-1, keepdims=True) + 1e-06) * gains


def norm_grad(values, gains, upstream):
    return jax.vjp(rms_norm, values, gains)[1](upstream)


def gelu_grad(values, upstream):
    return jax.vjp(jax.nn.gelu, values)[1](upstream)[0]


def split_heads(values):
    return values.reshape(values.shape[0], HEADS, HEAD)


def attend_scores(queries, keys, allowed):
    scores = jnp.einsum(
        "qhd,khd->hqk", split_heads(queries), split_heads(keys), preferred_element_type=jnp.float32
    )
    return jnp.where(allowed[None], scores * HEAD ** (-0.5), -1e30)


def attend_forward(queries, keys, values, allowed):
    scores = attend_scores(queries, keys, allowed)
    top = jnp.max(scores, axis=-1, keepdims=True)
    total = jnp.sum(jnp.exp(scores - top), axis=-1, keepdims=True)
    weights = jnp.exp(scores - top) / total
    mixed = jnp.einsum(
        "hqk,khd->qhd",
        weights.astype(jnp.bfloat16),
        split_heads(values),
        preferred_element_type=jnp.float32,
    )
    return (mixed.reshape(queries.shape[0], D).astype(jnp.bfloat16), top + jnp.log(total))


def attend_backward(queries, keys, values, allowed, log_total, grad_mixed):
    weights = jnp.exp(attend_scores(queries, keys, allowed) - log_total)
    grad_split = split_heads(grad_mixed)
    grad_weights = jnp.einsum(
        "qhd,khd->hqk", grad_split, split_heads(values), preferred_element_type=jnp.float32
    )
    grad_scores = weights * (grad_weights - jnp.sum(grad_weights * weights, axis=-1, keepdims=True))
    grad_low = grad_scores.astype(jnp.bfloat16)
    grad_q = jnp.einsum(
        "hqk,khd->qhd", grad_low, split_heads(keys), preferred_element_type=jnp.float32
    ) * HEAD ** (-0.5)
    grad_k = jnp.einsum(
        "hqk,qhd->khd", grad_low, split_heads(queries), preferred_element_type=jnp.float32
    ) * HEAD ** (-0.5)
    grad_v = jnp.einsum(
        "hqk,qhd->khd", weights.astype(jnp.bfloat16), grad_split, preferred_element_type=jnp.float32
    )
    return (
        grad_q.reshape(queries.shape[0], D),
        grad_k.reshape(keys.shape[0], D),
        grad_v.reshape(keys.shape[0], D),
    )


def adapter_forward(branch, down, upward):
    inner = matmul(branch, down) * D ** (-0.5)
    active = jax.nn.gelu(inner).astype(jnp.bfloat16)
    return (branch.astype(jnp.float32) + matmul(active, upward) * ADAPT ** (-0.5), inner, active)


def adapter_backward(branch, down, upward, inner, active, grad_out):
    grad_low = grad_out.astype(jnp.bfloat16)
    grad_up = matmul_left_t(active, grad_low) * ADAPT ** (-0.5)
    grad_active = matmul_right_t(grad_low, upward) * ADAPT ** (-0.5)
    grad_inner = gelu_grad(inner, grad_active).astype(jnp.bfloat16)
    grad_down = matmul_left_t(branch, grad_inner) * D ** (-0.5)
    grad_branch = grad_out + matmul_right_t(grad_inner, down) * D ** (-0.5)
    return (grad_branch.astype(jnp.bfloat16), grad_down, grad_up)


def split_params(generated):
    values = generated.astype(jnp.float32)
    gains = tuple((1.0 + 0.25 * values[k * D : (k + 1) * D] for k in range(3)))
    block = D * ADAPT
    start = 3 * D
    down_first = generated[start : start + block].reshape(D, ADAPT)
    up_first = generated[start + block : start + 2 * block].reshape(ADAPT, D)
    down_second = generated[start + 2 * block : start + 3 * block].reshape(D, ADAPT)
    up_second = generated[start + 3 * block : start + 4 * block].reshape(ADAPT, D)
    return (gains, down_first, up_first, down_second, up_second)


def by_owner(values, owners):
    return values.reshape((owners, values.shape[0] // owners) + values.shape[1:])


def shards(
    tokens,
    memory,
    target_lengths,
    memory_lengths,
    task_ids,
    cotangent,
    self_qkv,
    self_out,
    cross_q,
    cross_kv,
    cross_out,
    ffn_in,
    ffn_out,
    task_table,
    hyper_in,
    hyper_gen,
):
    forward_full = (
        lax.all_gather(self_qkv, "fsdp", axis=0, tiled=True),
        lax.all_gather(self_out, "fsdp", axis=0, tiled=True),
        lax.all_gather(cross_q, "fsdp", axis=0, tiled=True),
        lax.all_gather(cross_kv, "fsdp", axis=0, tiled=True),
        lax.all_gather(cross_out, "fsdp", axis=0, tiled=True),
        lax.all_gather(ffn_in, "fsdp", axis=0, tiled=True),
        lax.all_gather(ffn_out, "fsdp", axis=0, tiled=True),
    )
    w_qkv, w_sout, w_cq, w_ckv, w_cout, w_in, w_out = forward_full
    select = (jnp.arange(TASKS, dtype=jnp.int32) == task_ids[0]).astype(jnp.float32)
    pre_all = jnp.dot(task_table, hyper_in, precision=lax.Precision.HIGHEST)
    hidden_all = jax.nn.gelu(pre_all).astype(jnp.bfloat16)
    gen_shard = matmul(hidden_all, hyper_gen).astype(jnp.bfloat16)
    gen_tasks = lax.all_gather(gen_shard, "fsdp", axis=1, tiled=True)
    generated = matmul(select.astype(jnp.bfloat16)[None, :], gen_tasks)[0].astype(jnp.bfloat16)
    gains, down_first, up_first, down_second, up_second = split_params(generated)
    token_rows = tokens.shape[0]
    target_len = target_lengths[0]
    positions = jnp.arange(token_rows, dtype=jnp.int32)
    valid = (positions < target_len)[:, None]
    self_allowed = (positions[None, :] <= positions[:, None]) & (positions[None, :] < target_len)
    slots = jnp.arange(memory.shape[0], dtype=jnp.int32)
    memory_allowed = jnp.broadcast_to(
        (slots < memory_lengths[0])[None, :], (token_rows, memory.shape[0])
    )
    inputs = tokens.astype(jnp.float32)
    normed_self = rms_norm(inputs, gains[0]).astype(jnp.bfloat16)
    qkv = matmul(normed_self, w_qkv).astype(jnp.bfloat16)
    mixed_self, log_self = attend_forward(
        qkv[:, :D], qkv[:, D : 2 * D], qkv[:, 2 * D :], self_allowed
    )
    branch_self = matmul(mixed_self, w_sout).astype(jnp.bfloat16)
    adapted_self, inner_self, active_self = adapter_forward(branch_self, down_first, up_first)
    first = inputs + adapted_self
    normed_cross = rms_norm(first, gains[1]).astype(jnp.bfloat16)
    cross_queries = matmul(normed_cross, w_cq).astype(jnp.bfloat16)
    memory_kv = matmul(memory, w_ckv).astype(jnp.bfloat16)
    mixed_cross, log_cross = attend_forward(
        cross_queries, memory_kv[:, :D], memory_kv[:, D:], memory_allowed
    )
    second = first + matmul(mixed_cross, w_cout)
    normed_ffn = rms_norm(second, gains[2]).astype(jnp.bfloat16)
    pre_ffn = matmul(normed_ffn, w_in)
    hidden_ffn = jax.nn.gelu(pre_ffn).astype(jnp.bfloat16)
    branch_ffn = matmul(hidden_ffn, w_out).astype(jnp.bfloat16)
    adapted_ffn, inner_ffn, active_ffn = adapter_forward(branch_ffn, down_second, up_second)
    result = second + adapted_ffn
    mixed_out = jnp.where(valid, result, 0.0).astype(jnp.bfloat16)
    back_full = (
        lax.all_gather(self_qkv, "fsdp", axis=0, tiled=True),
        lax.all_gather(self_out, "fsdp", axis=0, tiled=True),
        lax.all_gather(cross_q, "fsdp", axis=0, tiled=True),
        lax.all_gather(cross_kv, "fsdp", axis=0, tiled=True),
        lax.all_gather(cross_out, "fsdp", axis=0, tiled=True),
        lax.all_gather(ffn_in, "fsdp", axis=0, tiled=True),
        lax.all_gather(ffn_out, "fsdp", axis=0, tiled=True),
    )
    w_qkv, w_sout, w_cq, w_ckv, w_cout, w_in, w_out = back_full
    grad_result = jnp.where(valid, cotangent.astype(jnp.float32), 0.0)
    grad_branch_ffn, grad_down_second, grad_up_second = adapter_backward(
        branch_ffn, down_second, up_second, inner_ffn, active_ffn, grad_result
    )
    grad_ffn_out = matmul_left_t(hidden_ffn, grad_branch_ffn)
    grad_pre = gelu_grad(pre_ffn, matmul_right_t(grad_branch_ffn, w_out)).astype(jnp.bfloat16)
    grad_ffn_in = matmul_left_t(normed_ffn, grad_pre)
    grad_part, grad_gain_third = norm_grad(second, gains[2], matmul_right_t(grad_pre, w_in))
    grad_second = grad_result + grad_part
    grad_cross_branch = grad_second.astype(jnp.bfloat16)
    grad_cross_out = matmul_left_t(mixed_cross, grad_cross_branch)
    grad_mixed_cross = matmul_right_t(grad_cross_branch, w_cout).astype(jnp.bfloat16)
    grad_q2, grad_k2, grad_v2 = attend_backward(
        cross_queries,
        memory_kv[:, :D],
        memory_kv[:, D:],
        memory_allowed,
        log_cross,
        grad_mixed_cross,
    )
    grad_queries = grad_q2.astype(jnp.bfloat16)
    grad_memory_kv = jnp.concatenate([grad_k2, grad_v2], axis=1).astype(jnp.bfloat16)
    grad_cross_q = matmul_left_t(normed_cross, grad_queries)
    grad_cross_kv = matmul_left_t(memory, grad_memory_kv)
    memory_grad = matmul_right_t(grad_memory_kv, w_ckv)
    grad_part, grad_gain_second = norm_grad(first, gains[1], matmul_right_t(grad_queries, w_cq))
    grad_first = grad_second + grad_part
    grad_branch_self, grad_down_first, grad_up_first = adapter_backward(
        branch_self, down_first, up_first, inner_self, active_self, grad_first
    )
    grad_self_out = matmul_left_t(mixed_self, grad_branch_self)
    grad_mixed_self = matmul_right_t(grad_branch_self, w_sout).astype(jnp.bfloat16)
    grad_q1, grad_k1, grad_v1 = attend_backward(
        qkv[:, :D], qkv[:, D : 2 * D], qkv[:, 2 * D :], self_allowed, log_self, grad_mixed_self
    )
    grad_qkv = jnp.concatenate([grad_q1, grad_k1, grad_v1], axis=1).astype(jnp.bfloat16)
    grad_self_qkv = matmul_left_t(normed_self, grad_qkv)
    grad_part, grad_gain_first = norm_grad(inputs, gains[0], matmul_right_t(grad_qkv, w_qkv))
    token_grad = grad_first + grad_part
    grad_generated = jnp.concatenate(
        [
            0.25 * grad_gain_first,
            0.25 * grad_gain_second,
            0.25 * grad_gain_third,
            grad_down_first.reshape(-1),
            grad_up_first.reshape(-1),
            grad_down_second.reshape(-1),
            grad_up_second.reshape(-1),
        ]
    ).astype(jnp.bfloat16)
    owners = lax.axis_size("fsdp")
    generated_pieces = grad_generated.astype(jnp.float32).reshape(
        owners, grad_generated.shape[0] // owners
    )
    tasks_term = select[None, :, None] * generated_pieces[:, None, :]
    pieces = (
        lax.all_to_all(
            by_owner(grad_self_qkv, owners).astype(jnp.bfloat16),
            "fsdp",
            split_axis=0,
            concat_axis=0,
            tiled=True,
        ).astype(jnp.float32),
        lax.all_to_all(
            by_owner(grad_self_out, owners).astype(jnp.bfloat16),
            "fsdp",
            split_axis=0,
            concat_axis=0,
            tiled=True,
        ).astype(jnp.float32),
        lax.all_to_all(
            by_owner(grad_cross_q, owners).astype(jnp.bfloat16),
            "fsdp",
            split_axis=0,
            concat_axis=0,
            tiled=True,
        ).astype(jnp.float32),
        lax.all_to_all(
            by_owner(grad_cross_kv, owners).astype(jnp.bfloat16),
            "fsdp",
            split_axis=0,
            concat_axis=0,
            tiled=True,
        ).astype(jnp.float32),
        lax.all_to_all(
            by_owner(grad_cross_out, owners).astype(jnp.bfloat16),
            "fsdp",
            split_axis=0,
            concat_axis=0,
            tiled=True,
        ).astype(jnp.float32),
        lax.all_to_all(
            by_owner(grad_ffn_in, owners).astype(jnp.bfloat16),
            "fsdp",
            split_axis=0,
            concat_axis=0,
            tiled=True,
        ).astype(jnp.float32),
        lax.all_to_all(
            by_owner(grad_ffn_out, owners).astype(jnp.bfloat16),
            "fsdp",
            split_axis=0,
            concat_axis=0,
            tiled=True,
        ).astype(jnp.float32),
        lax.all_to_all(
            tasks_term.astype(jnp.bfloat16), "fsdp", split_axis=0, concat_axis=0, tiled=True
        ).astype(tasks_term.dtype),
    )
    summed = tuple((jnp.sum(piece, axis=0) for piece in pieces))
    task_grad_shard = summed[7]
    hyper_part = jnp.dot(
        hidden_all.astype(jnp.float32).T, task_grad_shard, precision=lax.Precision.HIGHEST
    )
    grad_hidden_tasks = jnp.dot(
        task_grad_shard, hyper_gen.astype(jnp.float32).T, precision=lax.Precision.HIGHEST
    )
    grouped = (
        lax.psum(summed[0].astype(jnp.bfloat16), "dp").astype(jnp.float32),
        lax.psum(summed[1].astype(jnp.bfloat16), "dp").astype(jnp.float32),
        lax.psum(summed[2].astype(jnp.bfloat16), "dp").astype(jnp.float32),
        lax.psum(summed[3].astype(jnp.bfloat16), "dp").astype(jnp.float32),
        lax.psum(summed[4].astype(jnp.bfloat16), "dp").astype(jnp.float32),
        lax.psum(summed[5].astype(jnp.bfloat16), "dp").astype(jnp.float32),
        lax.psum(summed[6].astype(jnp.bfloat16), "dp").astype(jnp.float32),
        lax.psum(hyper_part.astype(jnp.bfloat16), "dp").astype(jnp.float32),
    )
    grad_pre_all = gelu_grad(pre_all, grad_hidden_tasks)
    table_term = jnp.dot(grad_pre_all, hyper_in.T, precision=lax.Precision.HIGHEST)
    first_term = jnp.dot(task_table.T, grad_pre_all, precision=lax.Precision.HIGHEST)
    small_sums = lax.psum((table_term, first_term), ("dp", "fsdp"))
    return (
        mixed_out,
        token_grad,
        memory_grad,
        grouped[0],
        grouped[1],
        grouped[2],
        grouped[3],
        grouped[4],
        grouped[5],
        grouped[6],
        small_sums[0],
        small_sums[1],
        grouped[7],
    )


def solution(mesh):
    return jax.shard_map(
        shards,
        mesh=mesh,
        in_specs=(
            P(("dp", "fsdp"), None),
            P(("dp", "fsdp"), None),
            P(("dp", "fsdp")),
            P(("dp", "fsdp")),
            P(("dp", "fsdp")),
            P(("dp", "fsdp"), None),
            P("fsdp", None),
            P("fsdp", None),
            P("fsdp", None),
            P("fsdp", None),
            P("fsdp", None),
            P("fsdp", None),
            P("fsdp", None),
            P(),
            P(),
            P(None, "fsdp"),
        ),
        out_specs=(
            P(("dp", "fsdp"), None),
            P(("dp", "fsdp"), None),
            P(("dp", "fsdp"), None),
            P("fsdp", None),
            P("fsdp", None),
            P("fsdp", None),
            P("fsdp", None),
            P("fsdp", None),
            P("fsdp", None),
            P("fsdp", None),
            P(),
            P(),
            P(None, "fsdp"),
        ),
        check_vma=False,
    )
```

profile of v0, /device:TPU:0, one launch (start us, length us, event | category | flops | bytes accessed | tf_op | source)
XLA Modules:
  0.0 963.8 jit_solution(12195619606107054193)
XLA Ops:
  19.1 17.2 %all-gather.24.cloned.1.call-done = bf16[8,9504,8]{1,2,0:T(8,128)(2,1)} async-done(((bf16[1,9504,8]{1,2,0:T(8,128)(2,1)}), bf16[8,9504,8]{1,2,0:T(8,128)(2,1)}) %all-gather.24.cloned.1.call-update) | async-done | bytes 1216528 | tf_op jit(solution)/shard_map/all_gather | solution.py:154
  50.4 18.6 %all-gather.14.cloned.1.call-done = bf16[768,1536]{1,0:T(8,128)(2,1)} async-done(((bf16[96,1536]{1,0:T(8,128)(2,1)}), bf16[768,1536]{1,0:T(8,128)(2,1)}) %all-gather.14.cloned.1.call-update) | async-done | bytes 2359312 | tf_op jit(solution)/shard_map/all_gather | solution.py:144
  78.2 33.2 %all-gather.10.cloned.1.call-done = bf16[768,2304]{1,0:T(8,128)(2,1)} async-done(((bf16[96,2304]{1,0:T(8,128)(2,1)}), bf16[768,2304]{1,0:T(8,128)(2,1)}) %all-gather.10.cloned.1.call-update) | async-done | bytes 3538960 | tf_op jit(solution)/shard_map/all_gather | solution.py:141
  123.0 11.4 %all-gather.12.cloned.1.call-done = bf16[768,768]{1,0:T(8,128)(2,1)} async-done(((bf16[96,768]{1,0:T(8,128)(2,1)}), bf16[768,768]{1,0:T(8,128)(2,1)}) %all-gather.12.cloned.1.call-update) | async-done | bytes 1179664 | tf_op jit(solution)/shard_map/all_gather | solution.py:142
  138.5 19.9 %all-gather.16.cloned.1.call-done = bf16[768,768]{1,0:T(8,128)(2,1)} async-done(((bf16[96,768]{1,0:T(8,128)(2,1)}), bf16[768,768]{1,0:T(8,128)(2,1)}) %all-gather.16.cloned.1.call-update) | async-done | bytes 1179664 | tf_op jit(solution)/shard_map/all_gather | solution.py:143
  171.2 11.1 %all-gather.18.cloned.1.call-done = bf16[768,768]{1,0:T(8,128)(2,1)} async-done(((bf16[96,768]{1,0:T(8,128)(2,1)}), bf16[768,768]{1,0:T(8,128)(2,1)}) %all-gather.18.cloned.1.call-update) | async-done | bytes 1179664 | tf_op jit(solution)/shard_map/all_gather | solution.py:145
  185.7 49.8 %all-gather.20.cloned.1.call-done = bf16[768,3072]{1,0:T(8,128)(2,1)} async-done(((bf16[96,3072]{1,0:T(8,128)(2,1)}), bf16[768,3072]{1,0:T(8,128)(2,1)}) %all-gather.20.cloned.1.call-update) | async-done | bytes 4718608 | tf_op jit(solution)/shard_map/all_gather | solution.py:146
  235.5 5.5 fusion.114
  241.0 46.7 %all-gather.22.cloned.1.call-done = bf16[3072,768]{1,0:T(8,128)(2,1)} async-done(((bf16[384,768]{1,0:T(8,128)(2,1)}), bf16[3072,768]{1,0:T(8,128)(2,1)}) %all-gather.22.cloned.1.call-update) | async-done | bytes 4718608 | tf_op jit(solution)/shard_map/all_gather | solution.py:147
  287.7 5.4 convolution_convert_fusion.13
  304.8 5.3 multiply_reduce_fusion
  326.6 4.3 all-to-all-start.2
  343.5 16.7 %all-to-all-done.2 = bf16[8,96,768]{2,1,0:T(8,128)(2,1)} async-done(((bf16[8,96,768]{2,1,0:T(8,128)(2,1)}), bf16[8,96,768]{2,1,0:T(8,128)(2,1)}, u32[]{:S(2)}, u32[]{:S(2)}) %all-to-all-start.2) | async-done | bytes 1179680 | tf_op jit(solution)/shard_map/all_to_all | solution.py:269
  360.3 4.3 all-to-all-start.4
  393.9 4.3 all-to-all-start.1
  400.1 27.5 %all-to-all-done.1 = bf16[8,96,768]{2,1,0:T(8,128)(2,1)} async-done(((bf16[8,96,768]{2,1,0:T(8,128)(2,1)}), bf16[8,96,768]{2,1,0:T(8,128)(2,1)}, u32[]{:S(2)}, u32[]{:S(2)}) %all-to-all-start.1) | async-done | bytes 1179680 | tf_op jit(solution)/shard_map/all_to_all | solution.py:262
  427.6 4.5 all-to-all-start.7
  442.9 19.7 %all-to-all-done.7 = bf16[8,8,9504]{2,1,0:T(8,128)(2,1)} async-done(((bf16[8,8,9504]{2,1,0:T(8,128)(2,1)}), bf16[8,8,9504]{2,1,0:T(8,128)(2,1)}, u32[]{:S(2)}, u32[]{:S(2)}) %all-to-all-start.7) | async-done | bytes 1216544 | tf_op jit(solution)/shard_map/all_to_all | solution.py:304
  462.5 4.4 all-to-all-start.3
  467.0 4.4 convolution_convert_fusion.4
  471.4 50.3 %all-to-all-done.3 = bf16[8,96,1536]{2,1,0:T(8,128)(2,1)} async-done(((bf16[8,96,1536]{2,1,0:T(8,128)(2,1)}), bf16[8,96,1536]{2,1,0:T(8,128)(2,1)}, u32[]{:S(2)}, u32[]{:S(2)}) %all-to-all-start.3) | async-done | bytes 2359328 | tf_op jit(solution)/shard_map/all_to_all | solution.py:276
  521.6 4.6 all-to-all-start
  526.3 5.1 convolution_convert_fusion.3
  531.4 74.8 %all-to-all-done = bf16[8,96,2304]{2,1,0:T(8,128)(2,1)} async-done(((bf16[8,96,2304]{2,1,0:T(8,128)(2,1)}), bf16[8,96,2304]{2,1,0:T(8,128)(2,1)}, u32[]{:S(2)}, u32[]{:S(2)}) %all-to-all-start) | async-done | bytes 3538976 | tf_op jit(solution)/shard_map/all_to_all | solution.py:255
  606.2 4.6 all-to-all-start.5
  610.9 6.4 convolution_convert_fusion.2
  617.2 98.9 %all-to-all-done.5 = bf16[8,96,3072]{2,1,0:T(8,128)(2,1)} async-done(((bf16[8,96,3072]{2,1,0:T(8,128)(2,1)}), bf16[8,96,3072]{2,1,0:T(8,128)(2,1)}, u32[]{:S(2)}, u32[]{:S(2)}) %all-to-all-start.5) | async-done | bytes 4718624 | tf_op jit(solution)/shard_map/all_to_all | solution.py:290
  716.1 4.6 all-to-all-start.6
  728.6 5.5 convolution_convert_fusion
  744.5 81.5 %all-to-all-done.6 = bf16[8,384,768]{2,1,0:T(8,128)(2,1)} async-done(((bf16[8,384,768]{2,1,0:T(8,128)(2,1)}), bf16[8,384,768]{2,1,0:T(8,128)(2,1)}, u32[]{:S(2)}, u32[]{:S(2)}) %all-to-all-start.6) | async-done | bytes 4718624 | tf_op jit(solution)/shard_map/all_to_all | solution.py:297
  840.2 38.7 %all-reduce = (f32[8,64]{1,0:T(8,128)}, f32[64,128]{1,0:T(8,128)}) all-reduce(f32[8,64]{1,0:T(8,128)S(1)} %fusion.111, f32[64,128]{1,0:T(8,128)S(1)} %convolution_bitcast_fusion), channel_id=1, replica_groups=mesh['dp'=4,'fsdp'=8] {'dp','fsdp'}, use_global_device_ids=true, to_apply=%region_30.31 | all-reduce | flops 8704 | bytes 69632 | tf_op jit(solution)/shard_map/psum | solution.py:329
  878.9 67.9 %all-reduce.4.cloned.1.call-done = (bf16[96,2304]{1,0:T(8,128)(2,1)}, bf16[96,768]{1,0:T(8,128)(2,1)}, bf16[96,768]{1,0:T(8,128)(2,1)}, bf16[96,1536]{1,0:T(8,12...) async-done(((bf16[96,2304]{1,0:T(8,128)(2,1)}, bf16[96,768]{1,0:T(8,128)(2,1)}, ...) | async-done | bytes 4792336 | tf_op jit(solution)/shard_map/psum | solution.py:317
  (324 shorter events, 189.5 us)
Async XLA Ops:
  7.2 29.1 %all-gather.24.cloned.1.call-start = ((), (), s32[]{:S(2)}) async-start(), calls=%async_computation.15 | async-start | bytes 1382400 | tf_op jit(solution)/shard_map/all_gather | solution.py:154
  10.3 58.7 %all-gather.14.cloned.1.call-start = ((), (), s32[]{:S(2)}) async-start(), calls=%async_computation.10 | async-start | bytes 2654208 | tf_op jit(solution)/shard_map/all_gather | solution.py:144
  11.1 100.3 %all-gather.10.cloned.1.call-start = ((), (), s32[]{:S(2)}) async-start(), calls=%async_computation.8 | async-start | bytes 3981312 | tf_op jit(solution)/shard_map/all_gather | solution.py:141
  11.8 122.6 %all-gather.12.cloned.1.call-start = ((), (), s32[]{:S(2)}) async-start(), calls=%async_computation.9 | async-start | bytes 1327104 | tf_op jit(solution)/shard_map/all_gather | solution.py:142
  12.4 146.0 %all-gather.16.cloned.1.call-start = ((), (), s32[]{:S(2)}) async-start(), calls=%async_computation.11 | async-start | bytes 1327104 | tf_op jit(solution)/shard_map/all_gather | solution.py:143
  13.0 169.3 %all-gather.18.cloned.1.call-start = ((), (), s32[]{:S(2)}) async-start(), calls=%async_computation.12 | async-start | bytes 1327104 | tf_op jit(solution)/shard_map/all_gather | solution.py:145
  13.6 221.9 %all-gather.20.cloned.1.call-start = ((), (), s32[]{:S(2)}) async-start(), calls=%async_computation.13 | async-start | bytes 5308416 | tf_op jit(solution)/shard_map/all_gather | solution.py:146
  14.3 273.4 %all-gather.22.cloned.1.call-start = ((), (), s32[]{:S(2)}) async-start(), calls=%async_computation.14 | async-start | bytes 5308416 | tf_op jit(solution)/shard_map/all_gather | solution.py:147
  15.2 31.0 %copy-start.67 = (f32[256]{0:T(256)}, f32[256]{0:T(256)S(1)}, u32[]{:S(2)}) copy-start(f32[256]{0:T(256)S(1)} %fusion.57) | copy-start | bytes 3076
  15.3 96.1 %copy-start.76 = (f32[256]{0:T(256)}, f32[256]{0:T(256)S(1)}, u32[]{:S(2)}) copy-start(f32[256]{0:T(256)S(1)} %fusion.99) | copy-start | bytes 3076
  15.9 30.3 %copy-start.72 = (pred[256]{0:T(512)(128)(4,1)}, pred[256]{0:T(512)(128)(4,1)S(1)}, u32[]{:S(2)}) copy-start(pred[256]{0:T(512)(128)(4,1)S(1)} %iota_compare_fusion.2) | copy-start | bytes 772
  50.4 60.9 %copy-start.60 = (f32[768]{0:T(1024)}, f32[768]{0:T(1024)S(1)}, u32[]{:S(2)}) copy-start(f32[768]{0:T(1024)S(1)} %get-tuple-element.38) | copy-start | bytes 9220
  123.0 13.2 %copy-start.42 = (bf16[12,64,256]{2,1,0:T(8,128)(2,1)}, bf16[12,64,256]{2,1,0:T(8,128)(2,1)S(1)}, u32[]{:S(2)}) copy-start(bf16[12,64,256]{2,1,0:T(8,128)(2,1)S(1)} %fusion.33) | copy-start | bytes 1179652
  136.2 26.6 %copy-start.81 = (pred[512]{0:T(512)(128)(4,1)S(1)}, pred[512]{0:T(512)(128)(4,1)}, u32[]{:S(2)}) copy-start(pred[512]{0:T(512)(128)(4,1)} %iota_compare_fusion.1) | copy-start | bytes 1540
  138.5 24.4 %copy-start.70 = (f32[256]{0:T(256)}, f32[256]{0:T(256)S(1)}, u32[]{:S(2)}) copy-start(f32[256]{0:T(256)S(1)} %get-tuple-element.45) | copy-start | bytes 3076
  138.5 26.8 %copy-start.6 = (f32[256,768]{1,0:T(8,128)}, f32[256,768]{1,0:T(8,128)S(1)}, u32[]{:S(2)}) copy-start(f32[256,768]{1,0:T(8,128)S(1)} %get-tuple-element.46) | copy-start | bytes 2359300
  138.5 24.4 %copy-start.63 = (f32[256]{0:T(256)}, f32[256]{0:T(256)S(1)}, u32[]{:S(2)}) copy-start(f32[256]{0:T(256)S(1)} %fusion.100) | copy-start | bytes 3076
  241.0 52.9 %copy-start.73 = (pred[256]{0:T(512)(128)(4,1)S(1)}, pred[256]{0:T(512)(128)(4,1)}, u32[]{:S(2)}) copy-start(pred[256]{0:T(512)(128)(4,1)} %copy-done.72) | copy-start | bytes 772
  320.1 11.9 %copy-start.53 = (f32[256,24]{0,1:T(8,128)S(1)}, f32[256,24]{0,1:T(8,128)}, u32[]{:S(2)}) copy-start(f32[256,24]{0,1:T(8,128)} %copy-done.52) | copy-start | bytes 73732
  320.1 11.9 %copy-start.75 = (pred[256]{0:T(512)(128)(4,1)S(1)}, pred[256]{0:T(512)(128)(4,1)}, u32[]{:S(2)}) copy-start(pred[256]{0:T(512)(128)(4,1)} %copy-done.72) | copy-start | bytes 772
  326.6 33.7 %all-to-all-start.2 = ((bf16[8,96,768]{2,1,0:T(8,128)(2,1)}), bf16[8,96,768]{2,1,0:T(8,128)(2,1)}, u32[]{:S(2)}, u32[]{:S(2)}) async-start(bf16[8,96,768]{2,1,0:T(8,128)(2,1)} %convolution_convert_fusion.9), calls=%async_computation.2 | async-start | bytes 2359296 | tf_op jit(solution)/shard_map/all_to_all | solution.py:269
  340.9 23.6 %copy-start.66 = (bf16[256,24]{0,1:T(8,128)(2,1)S(1)}, bf16[256,24]{0,1:T(8,128)(2,1)}, u32[]{:S(2)}) copy-start(bf16[256,24]{0,1:T(8,128)(2,1)} %copy-done.65) | copy-start | bytes 36868
  360.3 33.7 %all-to-all-start.4 = ((bf16[8,96,768]{2,1,0:T(8,128)(2,1)}), bf16[8,96,768]{2,1,0:T(8,128)(2,1)}, u32[]{:S(2)}, u32[]{:S(2)}) async-start(bf16[8,96,768]{2,1,0:T(8,128)(2,1)} %convolution_convert_fusion.8), calls=%async_computation.4 | async-start | bytes 2359296 | tf_op jit(solution)/shard_map/all_to_all | solution.py:283
  393.9 33.7 %all-to-all-start.1 = ((bf16[8,96,768]{2,1,0:T(8,128)(2,1)}), bf16[8,96,768]{2,1,0:T(8,128)(2,1)}, u32[]{:S(2)}, u32[]{:S(2)}) async-start(bf16[8,96,768]{2,1,0:T(8,128)(2,1)} %convolution_convert_fusion.10), calls=%async_computation.1 | async-start | bytes 2359296 | tf_op jit(solution)/shard_map/all_to_all | solution.py:262
  427.6 34.9 %all-to-all-start.7 = ((bf16[8,8,9504]{2,1,0:T(8,128)(2,1)}), bf16[8,8,9504]{2,1,0:T(8,128)(2,1)}, u32[]{:S(2)}, u32[]{:S(2)}) async-start(bf16[8,8,9504]{2,1,0:T(8,128)(2,1)} %multiply_convert_fusion.3), calls=%async_computation.7 | async-start | bytes 2457600 | tf_op jit(solution)/shard_map/all_to_all | solution.py:304
  442.9 24.1 %copy-start.62 = (f32[768]{0:T(1024)S(1)}, f32[768]{0:T(1024)}, u32[]{:S(2)}) copy-start(f32[768]{0:T(1024)} %copy-done.60) | copy-start | bytes 9220
  442.9 24.1 %copy-start.78 = (f32[256]{0:T(256)S(1)}, f32[256]{0:T(256)}, u32[]{:S(2)}) copy-start(f32[256]{0:T(256)} %copy-done.76) | copy-start | bytes 3076
  462.5 59.1 %all-to-all-start.3 = ((bf16[8,96,1536]{2,1,0:T(8,128)(2,1)}), bf16[8,96,1536]{2,1,0:T(8,128)(2,1)}, u32[]{:S(2)}, u32[]{:S(2)}) async-start(bf16[8,96,1536]{2,1,0:T(8,128)(2,1)} %bitcast.183), calls=%async_computation.3 | async-start | bytes 4718592 | tf_op jit(solution)/shard_map/all_to_all | solution.py:276
  521.6 84.6 %all-to-all-start = ((bf16[8,96,2304]{2,1,0:T(8,128)(2,1)}), bf16[8,96,2304]{2,1,0:T(8,128)(2,1)}, u32[]{:S(2)}, u32[]{:S(2)}) async-start(bf16[8,96,2304]{2,1,0:T(8,128)(2,1)} %bitcast.170), calls=%async_computation | async-start | bytes 7077888 | tf_op jit(solution)/shard_map/all_to_all | solution.py:255
  606.2 109.9 %all-to-all-start.5 = ((bf16[8,96,3072]{2,1,0:T(8,128)(2,1)}), bf16[8,96,3072]{2,1,0:T(8,128)(2,1)}, u32[]{:S(2)}, u32[]{:S(2)}) async-start(bf16[8,96,3072]{2,1,0:T(8,128)(2,1)} %bitcast.161), calls=%async_computation.5 | async-start | bytes 9437184 | tf_op jit(solution)/shard_map/all_to_all | solution.py:290
  716.1 109.8 %all-to-all-start.6 = ((bf16[8,384,768]{2,1,0:T(8,128)(2,1)}), bf16[8,384,768]{2,1,0:T(8,128)(2,1)}, u32[]{:S(2)}, u32[]{:S(2)}) async-start(bf16[8,384,768]{2,1,0:T(8,128)(2,1)} %bitcast.167), calls=%async_computation.6 | async-start | bytes 9437184 | tf_op jit(solution)/shard_map/all_to_all | solution.py:297
  720.7 226.1 %all-reduce.4.cloned.1.call-start = ((), (), s32[]{:S(2)}) async-start(), calls=%async_computation.16 | async-start | bytes 9584640 | tf_op jit(solution)/shard_map/psum | solution.py:317
  (76 other events, 278.6 us)
Sparse Core Ops, SparseCore 0:
  10.5 25.7 all-gather.23
  37.9 31.0 all-gather.13
  70.7 40.6 all-gather.9
  112.9 21.5 all-gather.11
  135.9 22.4 all-gather.15
  159.9 22.4 all-gather.17
  184.0 51.4 all-gather.19
  237.1 50.5 all-gather.21
  830.1 116.6 all-reduce.3
where the time goes:
time: 976 us; the launch traced here: 964 us
  waiting for transfers between devices  651 us (67%)
  matrix products  118 us (12%)
  local copies, waits for them, and re-layouts  57.6 us (6%)
  other arithmetic  46.1 us (5%)
  blocking collectives  38.7 us (4%)
  starting transfers between devices  35.8 us (4%)
  between operations  17.4 us (2%)
    all_to_all x1, waiting for transfers between devices, shards(): lax.all_to_all(by_owner(grad_ffn_in, owners).astype(jnp.bfloat16), 'fsdp'...  98.9 us
    all_to_all x1, waiting for transfers between devices, shards(): lax.all_to_all(by_owner(grad_ffn_out, owners).astype(jnp.bfloat16), 'fsdp...  81.5 us
    all_to_all x1, waiting for transfers between devices, shards(): lax.all_to_all(by_owner(grad_self_qkv, owners).astype(jnp.bfloat16), 'fsd...  74.8 us
    psum x1, waiting for transfers between devices, shards(): lax.psum(summed[0].astype(jnp.bfloat16), 'dp').astype(jnp.float32)  67.9 us
    all_to_all x1, waiting for transfers between devices, shards(): lax.all_to_all(by_owner(grad_cross_kv, owners).astype(jnp.bfloat16), 'fsd...  50.3 us
    all_gather x1, waiting for transfers between devices, shards(): lax.all_gather(ffn_in, 'fsdp', axis=0, tiled=True)  49.8 us
    all_gather x1, waiting for transfers between devices, shards(): lax.all_gather(ffn_out, 'fsdp', axis=0, tiled=True)  46.7 us
    psum x1, blocking collectives, shards(): small_sums = lax.psum((table_term, first_term), ('dp', 'fsdp'))  38.7 us
  transfers between devices with their start and end apart: 17, of which 17 were waited for; matrix products, arithmetic and copies ran while one was open for 17% of the time, Pallas kernels for 0%

commit v1 on v0

v1 whole, which is shorter than its diff:
```python
import functools

import jax
import jax.numpy as jnp
from jax import lax
from jax.experimental import pallas as pl
from jax.experimental.pallas import tpu as pltpu
from jax.sharding import PartitionSpec as P

D = 768
HEADS = 12
HEAD = 64
ADAPT = 24
TASKS = 8
BOTH = ("dp", "fsdp")


def matmul(left, right):
    return jnp.dot(left, right, preferred_element_type=jnp.float32)


def matmul_left_t(left, right):
    return lax.dot_general(
        left, right, (((0,), (0,)), ((), ())), preferred_element_type=jnp.float32
    )


def matmul_right_t(left, right):
    return lax.dot_general(
        left, right, (((1,), (1,)), ((), ())), preferred_element_type=jnp.float32
    )


def rms_norm(values, gains):
    return values * lax.rsqrt(jnp.mean(values * values, axis=-1, keepdims=True) + 1e-06) * gains


def norm_grad(values, gains, upstream):
    return jax.vjp(rms_norm, values, gains)[1](upstream)


def gelu_grad(values, upstream):
    return jax.vjp(jax.nn.gelu, values)[1](upstream)[0]


def split_heads(values):
    return values.reshape(values.shape[0], HEADS, HEAD)


def attend_scores(queries, keys, allowed):
    scores = jnp.einsum(
        "qhd,khd->hqk", split_heads(queries), split_heads(keys), preferred_element_type=jnp.float32
    )
    return jnp.where(allowed[None], scores * HEAD ** (-0.5), -1e30)


def attend_forward(queries, keys, values, allowed):
    scores = attend_scores(queries, keys, allowed)
    top = jnp.max(scores, axis=-1, keepdims=True)
    total = jnp.sum(jnp.exp(scores - top), axis=-1, keepdims=True)
    weights = jnp.exp(scores - top) / total
    mixed = jnp.einsum(
        "hqk,khd->qhd",
        weights.astype(jnp.bfloat16),
        split_heads(values),
        preferred_element_type=jnp.float32,
    )
    return (mixed.reshape(queries.shape[0], D).astype(jnp.bfloat16), top + jnp.log(total))


def attend_backward(queries, keys, values, allowed, log_total, grad_mixed):
    weights = jnp.exp(attend_scores(queries, keys, allowed) - log_total)
    grad_split = split_heads(grad_mixed)
    grad_weights = jnp.einsum(
        "qhd,khd->hqk", grad_split, split_heads(values), preferred_element_type=jnp.float32
    )
    grad_scores = weights * (grad_weights - jnp.sum(grad_weights * weights, axis=-1, keepdims=True))
    grad_low = grad_scores.astype(jnp.bfloat16)
    grad_q = jnp.einsum(
        "hqk,khd->qhd", grad_low, split_heads(keys), preferred_element_type=jnp.float32
    ) * HEAD ** (-0.5)
    grad_k = jnp.einsum(
        "hqk,qhd->khd", grad_low, split_heads(queries), preferred_element_type=jnp.float32
    ) * HEAD ** (-0.5)
    grad_v = jnp.einsum(
        "hqk,qhd->khd", weights.astype(jnp.bfloat16), grad_split, preferred_element_type=jnp.float32
    )
    return (
        grad_q.reshape(queries.shape[0], D),
        grad_k.reshape(keys.shape[0], D),
        grad_v.reshape(keys.shape[0], D),
    )


def adapter_forward(branch, down, upward):
    inner = matmul(branch, down) * D ** (-0.5)
    active = jax.nn.gelu(inner).astype(jnp.bfloat16)
    return (branch.astype(jnp.float32) + matmul(active, upward) * ADAPT ** (-0.5), inner, active)


def adapter_backward(branch, down, upward, inner, active, grad_out):
    grad_low = grad_out.astype(jnp.bfloat16)
    grad_up = matmul_left_t(active, grad_low) * ADAPT ** (-0.5)
    grad_active = matmul_right_t(grad_low, upward) * ADAPT ** (-0.5)
    grad_inner = gelu_grad(inner, grad_active).astype(jnp.bfloat16)
    grad_down = matmul_left_t(branch, grad_inner) * D ** (-0.5)
    grad_branch = grad_out + matmul_right_t(grad_inner, down) * D ** (-0.5)
    return (grad_branch.astype(jnp.bfloat16), grad_down, grad_up)


def split_params(generated):
    values = generated.astype(jnp.float32)
    gains = tuple((1.0 + 0.25 * values[k * D : (k + 1) * D] for k in range(3)))
    block = D * ADAPT
    start = 3 * D
    down_first = generated[start : start + block].reshape(D, ADAPT)
    up_first = generated[start + block : start + 2 * block].reshape(ADAPT, D)
    down_second = generated[start + 2 * block : start + 3 * block].reshape(D, ADAPT)
    up_second = generated[start + 3 * block : start + 4 * block].reshape(ADAPT, D)
    return (gains, down_first, up_first, down_second, up_second)


def moves(step):
    pairs = []
    for y in range(2):
        for x in range(2):
            for z in range(4):
                for c in range(2):
                    ty, tx, tz, tc = step(y, x, z, c)
                    pairs.append((((y * 2 + x) * 4 + z) * 2 + c, ((ty * 2 + tx) * 4 + tz) * 2 + tc))
    return pairs


def swap_x(values):
    return lax.ppermute(values, BOTH, moves(lambda y, x, z, c: (y, 1 - x, z, c)))


def swap_y(values):
    return lax.ppermute(values, BOTH, moves(lambda y, x, z, c: (1 - y, x, z, c)))


def swap_core(values):
    return lax.ppermute(values, BOTH, moves(lambda y, x, z, c: (y, x, z, 1 - c)))


def turn_z(values, by):
    return lax.ppermute(values, BOTH, moves(lambda y, x, z, c: (y, x, (z + by) % 4, c)))


def place_kernel(where, own, other, out, sems):
    q, z, c = where[0], where[1], where[2]
    copies = []
    for r in range(4):
        for k in range(4):
            for side, source in enumerate((own, other)):
                copies.append(
                    pltpu.make_async_copy(
                        source.at[r, k],
                        out.at[q ^ r, (z - k + 4) % 4, c ^ side],
                        sems.at[(r * 4 + k) * 2 + side],
                    )
                )
    for copy in copies:
        copy.start()
    for copy in copies:
        copy.wait()


def place(where, own, other):
    return pl.pallas_call(
        place_kernel,
        out_shape=jax.ShapeDtypeStruct((4, 4, 2) + own.shape[2:], own.dtype),
        grid_spec=pltpu.PrefetchScalarGridSpec(
            num_scalar_prefetch=1,
            grid=(1,),
            in_specs=[pl.BlockSpec(memory_space=pl.ANY)] * 2,
            out_specs=pl.BlockSpec(memory_space=pltpu.VMEM),
            scratch_shapes=[pltpu.SemaphoreType.DMA((32,))],
        ),
        compiler_params=pltpu.CompilerParams(vmem_limit_bytes=24 << 20),
        cost_estimate=pl.CostEstimate(flops=0, bytes_accessed=4 * own.size * own.dtype.itemsize, transcendentals=0),
        name="place",
    )(where, own, other)


def sort_kernel(where, blocks, keep, send, sems):
    q, z, c = where[0], where[1], where[2]
    copies = []
    for r in range(4):
        for k in range(4):
            for side, target in enumerate((keep, send)):
                copies.append(
                    pltpu.make_async_copy(
                        blocks.at[q ^ r, (z + k) % 4, c ^ side],
                        target.at[r, k],
                        sems.at[(r * 4 + k) * 2 + side],
                    )
                )
    for copy in copies:
        copy.start()
    for copy in copies:
        copy.wait()


def sort(where, blocks):
    half = jax.ShapeDtypeStruct((4, 4) + blocks.shape[3:], blocks.dtype)
    return pl.pallas_call(
        sort_kernel,
        out_shape=(half, half),
        grid_spec=pltpu.PrefetchScalarGridSpec(
            num_scalar_prefetch=1,
            grid=(1,),
            in_specs=[pl.BlockSpec(memory_space=pl.ANY)],
            out_specs=[pl.BlockSpec(memory_space=pltpu.VMEM)] * 2,
            scratch_shapes=[pltpu.SemaphoreType.DMA((32,))],
        ),
        compiler_params=pltpu.CompilerParams(vmem_limit_bytes=24 << 20),
        cost_estimate=pl.CostEstimate(flops=0, bytes_accessed=2 * blocks.size * blocks.dtype.itemsize, transcendentals=0),
        name="sort",
    )(where, blocks)


def gather_blocks(where, blocks, x_first):
    own = lax.dynamic_index_in_dim(jnp.stack(blocks), where[0], 0, keepdims=False)
    column = jnp.stack([own] + [turn_z(own, k) for k in (1, 2, 3)])
    if x_first:
        pair = jnp.stack([column, swap_x(column)])
        quad = jnp.concatenate([pair, swap_y(pair)])
    else:
        pair = jnp.stack([column, swap_y(column)])
        quad = jnp.stack([pair, swap_x(pair)], axis=1).reshape((4,) + column.shape)
    whole = place(where, quad, swap_core(quad))
    return whole.reshape(4, D, D)


def low(values):
    return values.astype(jnp.bfloat16)


def add_low(left, right):
    return low(left.astype(jnp.float32) + right.astype(jnp.float32))


def scatter_blocks(where, blocks, x_first):
    keep, send = sort(where, blocks.reshape(4, 4, 2, D // 8, D))
    total = add_low(keep, swap_core(send))
    if x_first:
        kept, sent = (total[0::2], total[1::2])
        total = add_low(kept, swap_x(sent))
        total = add_low(total[0], swap_y(total[1]))
    else:
        kept, sent = (total[:2], total[2:])
        total = add_low(kept, swap_y(sent))
        total = add_low(total[0], swap_x(total[1]))
    parts = [total[0]] + [turn_z(total[k], k) for k in (1, 2, 3)]
    parts = [part.astype(jnp.float32) for part in parts]
    own = low((parts[0] + parts[2]) + (parts[1] + parts[3]))
    pair = jnp.stack([own, swap_x(own)])
    quad = jnp.concatenate([pair, swap_y(pair)])
    return quad


def to_owner(where, quad):
    q = where[0]
    return [lax.dynamic_index_in_dim(quad, q ^ b, 0, keepdims=False).astype(jnp.float32) for b in range(4)]


def fast_transfers(
    task_id, self_qkv, self_out, cross_q, cross_kv, cross_out, ffn_in, ffn_out, hidden_all, hyper_gen
):
    q = lax.axis_index("dp").astype(jnp.int32)
    f = lax.axis_index("fsdp").astype(jnp.int32)
    where = jnp.stack([q, f // 2, f % 2])
    rows = self_qkv.shape[0]
    ids = jnp.stack([task_id, swap_core(task_id)])
    ids_ahead = [ids] + [turn_z(ids, 4 - k) for k in (1, 2, 3)]
    gen_shard = low(matmul(hidden_all, hyper_gen))

    def rows_of(tasks):
        select = low(tasks[:, None] == jnp.arange(TASKS, dtype=jnp.int32)[None, :])
        return low(matmul(select, gen_shard))

    asked = [rows_of(ids_ahead[k]) for k in range(4)]
    got = jnp.stack([asked[0]] + [turn_z(asked[k], k) for k in (1, 2, 3)], axis=1)
    pieces = jnp.concatenate([got[0], swap_core(got[1])])
    slots = jnp.arange(8, dtype=jnp.int32)
    source = ((slots % 2) ^ where[2]) * 4 + (where[1] - slots // 2 + 4) % 4
    unturn = low(source[:, None] == slots[None, :])
    generated = low(matmul(unturn, pieces)).reshape(-1)
    w1 = gather_blocks(
        where, [self_qkv[:, :D], self_qkv[:, D : 2 * D], self_qkv[:, 2 * D :], self_out], True
    )
    w2 = gather_blocks(where, [cross_q, cross_out, cross_kv[:, :D], cross_kv[:, D:]], False)
    w3 = gather_blocks(where, [ffn_in[:, b * D : (b + 1) * D] for b in range(4)], True)
    w4 = gather_blocks(where, [ffn_out[b * rows : (b + 1) * rows] for b in range(4)], False)
    return (where, ids_ahead, generated, w1, w2, w3, w4)


def layer(
    tokens,
    memory,
    target_len,
    memory_len,
    cotangent,
    generated,
    w_q,
    w_k,
    w_v,
    w_sout,
    w_cq,
    w_cout,
    w_ck,
    w_cv,
    w_in,
    w_out,
):
    w_qkv = jnp.concatenate([w_q, w_k, w_v], axis=1)
    w_ckv = jnp.concatenate([w_ck, w_cv], axis=1)
    w_in = jnp.concatenate(w_in, axis=1)
    w_out = jnp.concatenate(w_out, axis=0)
    gains, down_first, up_first, down_second, up_second = split_params(generated)
    token_rows = tokens.shape[0]
    positions = jnp.arange(token_rows, dtype=jnp.int32)
    valid = (positions < target_len)[:, None]
    self_allowed = (positions[None, :] <= positions[:, None]) & (positions[None, :] < target_len)
    slots = jnp.arange(memory.shape[0], dtype=jnp.int32)
    memory_allowed = jnp.broadcast_to((slots < memory_len)[None, :], (token_rows, memory.shape[0]))
    inputs = tokens.astype(jnp.float32)
    normed_self = low(rms_norm(inputs, gains[0]))
    qkv = low(matmul(normed_self, w_qkv))
    mixed_self, log_self = attend_forward(
        qkv[:, :D], qkv[:, D : 2 * D], qkv[:, 2 * D :], self_allowed
    )
    branch_self = low(matmul(mixed_self, w_sout))
    adapted_self, inner_self, active_self = adapter_forward(branch_self, down_first, up_first)
    first = inputs + adapted_self
    normed_cross = low(rms_norm(first, gains[1]))
    cross_queries = low(matmul(normed_cross, w_cq))
    memory_kv = low(matmul(memory, w_ckv))
    mixed_cross, log_cross = attend_forward(
        cross_queries, memory_kv[:, :D], memory_kv[:, D:], memory_allowed
    )
    second = first + matmul(mixed_cross, w_cout)
    normed_ffn = low(rms_norm(second, gains[2]))
    pre_ffn = matmul(normed_ffn, w_in)
    hidden_ffn = low(jax.nn.gelu(pre_ffn))
    branch_ffn = low(matmul(hidden_ffn, w_out))
    adapted_ffn, inner_ffn, active_ffn = adapter_forward(branch_ffn, down_second, up_second)
    result = second + adapted_ffn
    mixed_out = low(jnp.where(valid, result, 0.0))
    grad_result = jnp.where(valid, cotangent.astype(jnp.float32), 0.0)
    grad_branch_ffn, grad_down_second, grad_up_second = adapter_backward(
        branch_ffn, down_second, up_second, inner_ffn, active_ffn, grad_result
    )
    grad_ffn_out = low(matmul_left_t(hidden_ffn, grad_branch_ffn))
    grad_pre = low(gelu_grad(pre_ffn, matmul_right_t(grad_branch_ffn, w_out)))
    grad_ffn_in = low(matmul_left_t(normed_ffn, grad_pre))
    grad_part, grad_gain_third = norm_grad(second, gains[2], matmul_right_t(grad_pre, w_in))
    grad_second = grad_result + grad_part
    grad_cross_branch = low(grad_second)
    grad_cross_out = low(matmul_left_t(mixed_cross, grad_cross_branch))
    grad_mixed_cross = low(matmul_right_t(grad_cross_branch, w_cout))
    grad_q2, grad_k2, grad_v2 = attend_backward(
        cross_queries,
        memory_kv[:, :D],
        memory_kv[:, D:],
        memory_allowed,
        log_cross,
        grad_mixed_cross,
    )
    grad_queries = low(grad_q2)
    grad_memory_kv = low(jnp.concatenate([grad_k2, grad_v2], axis=1))
    grad_cross_q = low(matmul_left_t(normed_cross, grad_queries))
    grad_cross_kv = low(matmul_left_t(memory, grad_memory_kv))
    memory_grad = matmul_right_t(grad_memory_kv, w_ckv)
    grad_part, grad_gain_second = norm_grad(first, gains[1], matmul_right_t(grad_queries, w_cq))
    grad_first = grad_second + grad_part
    grad_branch_self, grad_down_first, grad_up_first = adapter_backward(
        branch_self, down_first, up_first, inner_self, active_self, grad_first
    )
    grad_self_out = low(matmul_left_t(mixed_self, grad_branch_self))
    grad_mixed_self = low(matmul_right_t(grad_branch_self, w_sout))
    grad_q1, grad_k1, grad_v1 = attend_backward(
        qkv[:, :D], qkv[:, D : 2 * D], qkv[:, 2 * D :], self_allowed, log_self, grad_mixed_self
    )
    grad_qkv = low(jnp.concatenate([grad_q1, grad_k1, grad_v1], axis=1))
    grad_self_qkv = low(matmul_left_t(normed_self, grad_qkv))
    grad_part, grad_gain_first = norm_grad(inputs, gains[0], matmul_right_t(grad_qkv, w_qkv))
    token_grad = grad_first + grad_part
    grad_generated = jnp.concatenate(
        [
            0.25 * grad_gain_first,
            0.25 * grad_gain_second,
            0.25 * grad_gain_third,
            grad_down_first.reshape(-1),
            grad_up_first.reshape(-1),
            grad_down_second.reshape(-1),
            grad_up_second.reshape(-1),
        ]
    ).astype(jnp.bfloat16)
    weight_grads = (
        grad_self_qkv,
        grad_self_out,
        grad_cross_q,
        grad_cross_kv,
        grad_cross_out,
        grad_ffn_in,
        grad_ffn_out,
    )
    return (mixed_out, token_grad, memory_grad, weight_grads, grad_generated)


def hyper_tail(task_grad, pre_all, hidden_all, task_table, hyper_in, hyper_gen, sum_owners):
    grad_hyper_gen = jnp.dot(
        hidden_all.astype(jnp.float32).T, task_grad, precision=lax.Precision.HIGHEST
    )
    grad_hidden = jnp.dot(
        task_grad, hyper_gen.astype(jnp.float32).T, precision=lax.Precision.HIGHEST
    )
    grad_pre_all = gelu_grad(pre_all, sum_owners(grad_hidden))
    grad_table = jnp.dot(grad_pre_all, hyper_in.T, precision=lax.Precision.HIGHEST)
    grad_first = jnp.dot(task_table.T, grad_pre_all, precision=lax.Precision.HIGHEST)
    return grad_table, grad_first, grad_hyper_gen


def columns_of(matrix):
    return [matrix[:, b * D : (b + 1) * D] for b in range(matrix.shape[1] // D)]


def rows_of_blocks(matrix):
    return [matrix[b * D : (b + 1) * D] for b in range(matrix.shape[0] // D)]


def shards(
    tokens,
    memory,
    target_lengths,
    memory_lengths,
    task_ids,
    cotangent,
    self_qkv,
    self_out,
    cross_q,
    cross_kv,
    cross_out,
    ffn_in,
    ffn_out,
    task_table,
    hyper_in,
    hyper_gen,
):
    owners = lax.axis_size("fsdp")
    buckets = lax.axis_size("dp")
    staged = owners == 8 and buckets == 4
    pre_all = jnp.dot(task_table, hyper_in, precision=lax.Precision.HIGHEST)
    hidden_all = low(jax.nn.gelu(pre_all))
    if staged:
        where, ids_ahead, generated, w1, w2, w3, w4 = fast_transfers(
            task_ids[0],
            self_qkv,
            self_out,
            cross_q,
            cross_kv,
            cross_out,
            ffn_in,
            ffn_out,
            hidden_all,
            hyper_gen,
        )
        w_in = list(w3)
        w_out = rows_of_blocks(w4.reshape(4, owners, -1, D).swapaxes(0, 1).reshape(-1, D))
        w_q, w_k, w_v, w_sout = w1
        w_cq, w_cout, w_ck, w_cv = w2
    else:
        full = [
            lax.all_gather(w, "fsdp", axis=0, tiled=True)
            for w in (self_qkv, self_out, cross_q, cross_kv, cross_out, ffn_in, ffn_out)
        ]
        w_q, w_k, w_v = columns_of(full[0])
        w_sout, w_cq = full[1], full[2]
        w_ck, w_cv = columns_of(full[3])
        w_cout = full[4]
        w_in, w_out = columns_of(full[5]), rows_of_blocks(full[6])
        select = low(task_ids[:, None] == jnp.arange(TASKS, dtype=jnp.int32)[None, :])
        gen_shard = low(matmul(hidden_all, hyper_gen))
        gen_tasks = lax.all_gather(gen_shard, "fsdp", axis=1, tiled=True)
        generated = low(matmul(select, gen_tasks)[0])
    mixed_out, token_grad, memory_grad, weight_grads, grad_generated = layer(
        tokens,
        memory,
        target_lengths[0],
        memory_lengths[0],
        cotangent,
        generated,
        w_q,
        w_k,
        w_v,
        w_sout,
        w_cq,
        w_cout,
        w_ck,
        w_cv,
        w_in,
        w_out,
    )
    g_qkv, g_sout, g_cq, g_ckv, g_cout, g_in, g_out = weight_grads
    if staged:
        s4 = to_owner(where, scatter_blocks(
            where, g_out.reshape(owners, 4, -1, D).swapaxes(0, 1).reshape(4, D, D), True
        ))
        s3 = to_owner(where, scatter_blocks(where, jnp.stack(columns_of(g_in)), False))
        s2 = to_owner(where, scatter_blocks(where, jnp.stack([g_cq, g_cout] + columns_of(g_ckv)), True))
        s1 = to_owner(where, scatter_blocks(where, jnp.stack(columns_of(g_qkv) + [g_sout]), False))
        summed = (
            jnp.concatenate(s1[:3], axis=1),
            s1[3],
            s2[0],
            jnp.concatenate(s2[2:], axis=1),
            s2[1],
            jnp.concatenate(s3, axis=1),
            jnp.concatenate(s4, axis=0),
        )
        z, c = where[1], where[2]
        pieces = grad_generated.reshape(4, 2, -1)
        mine = lax.dynamic_index_in_dim(pieces, c, 1, keepdims=False)
        theirs = lax.dynamic_index_in_dim(pieces, 1 - c, 1, keepdims=False)
        both = jnp.stack([mine, swap_core(theirs)], axis=1)
        both = [lax.dynamic_index_in_dim(both, (z + k) % 4, 0, keepdims=False) for k in range(4)]
        terms = jnp.concatenate([both[0]] + [turn_z(both[k], k) for k in (1, 2, 3)])
        ids = jnp.concatenate([ids_ahead[(4 - k) % 4] for k in range(4)])
        select = low(jnp.arange(TASKS, dtype=jnp.int32)[:, None] == ids[None, :])
        task_grad = low(matmul(select, terms))
        task_grad = add_low(task_grad, swap_x(task_grad))
        task_grad = task_grad.astype(jnp.float32) + swap_y(task_grad).astype(jnp.float32)

        def sum_owners(part):
            part = part + swap_core(part)
            turned = [part] + [turn_z(part, k) for k in (1, 2, 3)]
            return (turned[0] + turned[2]) + (turned[1] + turned[3])
    else:
        summed = tuple(
            lax.psum(low(lax.psum_scatter(g, "fsdp", scatter_dimension=0, tiled=True)), "dp").astype(
                jnp.float32
            )
            for g in weight_grads
        )
        pieces = grad_generated.reshape(owners, 1, -1)
        select = low(jnp.arange(TASKS, dtype=jnp.int32)[:, None] == task_ids[None, :])
        terms = low(select[None].astype(jnp.float32) * pieces.astype(jnp.float32))
        terms = lax.all_to_all(terms, "fsdp", split_axis=0, concat_axis=0, tiled=True)
        task_grad = low(jnp.sum(terms.astype(jnp.float32), axis=0))
        task_grad = lax.psum(task_grad, "dp").astype(jnp.float32)

        def sum_owners(part):
            return lax.psum(part, "fsdp")

    grad_table, grad_first, grad_hyper_gen = hyper_tail(
        task_grad, pre_all, hidden_all, task_table, hyper_in, hyper_gen, sum_owners
    )
    return (
        mixed_out,
        token_grad,
        memory_grad,
    ) + summed + (
        grad_table,
        grad_first,
        grad_hyper_gen,
    )


def solution(mesh):
    by_both = P(("dp", "fsdp"), None)
    by_rows = P("fsdp", None)
    return jax.shard_map(
        shards,
        mesh=mesh,
        in_specs=(by_both, by_both)
        + (P(("dp", "fsdp")),) * 3
        + (by_both,)
        + (by_rows,) * 7
        + (P(), P(), P(None, "fsdp")),
        out_specs=(by_both,) * 3 + (by_rows,) * 7 + (P(), P(), P(None, "fsdp")),
        check_vma=False,
    )
```

time: 976 us -> 512 us (0.52)
  waiting for transfers between devices: 651 us -> 169 us
  starting transfers between devices: 35.8 us -> 96.8 us
  Pallas kernels: 0 us -> 42.4 us
  blocking collectives: 38.7 us -> 0 us
  matrix products: 118 us -> 83 us
  between operations: 17.4 us -> 4.89 us
    all_to_all x8 -> x0, waiting for transfers between devices: 370 us -> none  [the longest x1 98.9 us: shards(): lax.all_to_all(by_owner(grad_ffn_in, owners).astype(jnp.bfloat16), 'fsdp'...]
    all_gather x8 -> x0, waiting for transfers between devices: 208 us -> none  [the longest x1 49.8 us: shards(): lax.all_gather(ffn_in, 'fsdp', axis=0, tiled=True)]
    ppermute x0 -> x74, waiting for transfers between devices: none -> 169 us  [the longest x13 87.9 us: swap_y(): lax.ppermute(values, BOTH, moves(lambda y, x, z, c: (1 - y, x, z, c)))]
    ppermute x0 -> x74, starting transfers between devices: none -> 96.8 us  [the longest x36 58.2 us: turn_z(): lax.ppermute(values, BOTH, moves(lambda y, x, z, c: (y, x, (z + by) % 4,...]
    psum x1 -> x0, waiting for transfers between devices: 67.9 us -> none  [shards(): lax.psum(summed[0].astype(jnp.bfloat16), 'dp').astype(jnp.float32)]
    pallas_call x0 -> x8, Pallas kernels: none -> 42.4 us  [the longest x4 29.5 us: sort(): pl.pallas_call(sort_kernel, out_shape=(half, half), grid_spec=pltpu.Prefe...]
    psum x1 -> x0, blocking collectives: 38.7 us -> none  [shards(): small_sums = lax.psum((table_term, first_term), ('dp', 'fsdp'))]
    all_to_all x8 -> x0, starting transfers between devices: 35.5 us -> none  [the longest x1 4.63 us: shards(): lax.all_to_all(by_owner(grad_ffn_in, owners).astype(jnp.bfloat16), 'fsdp'...]
  transfers between devices with their start and end apart: 17 -> 74, of which waited for: 17 -> 27; matrix products, arithmetic and copies ran while one was open for 17% -> 22% of each run, Pallas kernels for 0% -> 6%
where the time goes in v1:
time: 512 us; the launch traced here: 507 us
  waiting for transfers between devices  169 us (33%)
  starting transfers between devices  96.8 us (19%)
  matrix products  83 us (16%)
  local copies, waits for them, and re-layouts  65.8 us (13%)
  other arithmetic  44.9 us (9%)
  Pallas kernels  42.4 us (8%)
    ppermute x13, waiting for transfers between devices, swap_y(): lax.ppermute(values, BOTH, moves(lambda y, x, z, c: (1 - y, x, z, c)))  87.9 us
    ppermute x36, starting transfers between devices, turn_z(): lax.ppermute(values, BOTH, moves(lambda y, x, z, c: (y, x, (z + by) % 4,...  58.2 us
    ppermute x36, waiting for transfers between devices, turn_z(): lax.ppermute(values, BOTH, moves(lambda y, x, z, c: (y, x, (z + by) % 4,...  43.9 us
    ppermute x13, waiting for transfers between devices, swap_x(): lax.ppermute(values, BOTH, moves(lambda y, x, z, c: (y, 1 - x, z, c)))  36.8 us
    pallas_call x4, Pallas kernels, sort(): pl.pallas_call(sort_kernel, out_shape=(half, half), grid_spec=pltpu.Prefe...  29.5 us
    unnamed x227, local copies, waits for them, and re-layouts  24.9 us
    dot_general x11, matrix products, matmul_right_t(): lax.dot_general(left, right, (((1,), (1,)), ((), ())), preferred_element_...  23.6 us
    ppermute x13, starting transfers between devices, swap_x(): lax.ppermute(values, BOTH, moves(lambda y, x, z, c: (y, 1 - x, z, c)))  22.7 us
  transfers between devices with their start and end apart: 74, of which 27 were waited for; matrix products, arithmetic and copies ran while one was open for 22% of the time, Pallas kernels for 6%

profile of v1, /device:TPU:0, one launch (start us, length us, event | category | flops | bytes accessed | tf_op | source)
XLA Modules:
  0.0 507.1 jit_solution(4290091844918487402)
XLA Ops:
  2.7 5.1 %collective-permute-start.10 = (bf16[96,768]{1,0:T(8,128)(2,1)S(1)}, bf16[96,768]{1,0:T(8,128)(2,1)}, u32[]{:S(2)}, u32[]{:S(2)}) collective-permute-start(bf16[96,768]{1,0:T(8,128)(2,1)S(1)} %bitcast.441), channel_id=1, source_target_pairs={{0,6},{1,7},{2,0},{3,1},{4,2},{5,3},{6,4},{7,5},{8,14},{9,15},{10,... | collective-permute-start | bytes 442376 | tf_op jit(solution)/shard_map/ppermute | solution.py:147
  24.0 5.1 %collective-permute-done.5 = s32[2]{0:T(128)S(1)} collective-permute-done((s32[2]{0:T(128)S(1)}, s32[2]{0:T(128)S(1)}, u32[]{:S(2)}, u32[]{:S(2)}) %collective-permute-start.5) | collective-permute-done | bytes 40 | tf_op jit(solution)/shard_map/ppermute | solution.py:147
  29.4 4.3 collective-permute-done.3
  39.6 5.0 collective-permute-done.1
  52.7 7.4 %collective-permute-done.27 = bf16[96,768]{1,0:T(8,128)(2,1)S(1)} collective-permute-done((bf16[96,768]{1,0:T(8,128)(2,1)S(1)}, bf16[96,768]{1,0:T(8,128)(2,1)S(1)}, u32[]{:S(2)}, u32[]{:S(2)}) %collective-permute-start.27) | collective-permute-done | bytes 147488 | tf_op jit(solution)/shard_map/ppermute | solution.py:147
  61.1 3.9 collective-permute-start.6
  66.5 4.0 collective-permute-done.21
  77.1 10.3 %collective-permute-done.17 = bf16[4,96,768]{2,1,0:T(8,128)(2,1)S(1)} collective-permute-done((bf16[4,96,768]{2,1,0:T(8,128)(2,1)S(1)}, bf16[4,96,768]{2,1,0:T(8,128)(2,1)S(1)}, u32[]{:S(2)}, u32[]{:S(2)}) %collective-permute-start.17) | collective-permute-done | bytes 589856 | tf_op jit(solution)/shard_map/ppermute | solution.py:139
  91.4 8.7 %collective-permute-done.29 = bf16[4,96,768]{2,1,0:T(8,128)(2,1)S(1)} collective-permute-done((bf16[4,96,768]{2,1,0:T(8,128)(2,1)S(1)}, bf16[4,96,768]{2,1,0:T(8,128)(2,1)S(1)}, u32[]{:S(2)}, u32[]{:S(2)}) %collective-permute-start.29) | collective-permute-done | bytes 589856 | tf_op jit(solution)/shard_map/ppermute | solution.py:139
  106.6 18.7 %collective-permute-done.12 = bf16[2,4,96,768]{3,2,1,0:T(8,128)(2,1)S(1)} collective-permute-done((bf16[2,4,96,768]{3,2,1,0:T(8,128)(2,1)S(1)}, bf16[2,4,96,768]{3,2,1,0:T(8,128)(2,1)S(1)}, u32[]{:S(2)}, u32[]{:S(2)}) %collective-permute-start.12) | collective-permute-done | bytes 1179680 | tf_op jit(solution)/shard_map/ppermute | solution.py:139
  199.9 9.4 %fusion.9 = bf16[256,3072]{1,0:T(8,128)(2,1)S(1)} fusion(f32[256,3072]{1,0:T(8,128)S(1)} %fusion.56, bf16[256,768]{1,0:T(8,128)(2,1)S(1)} %fusion.33, bf16[768,768]{1,0:T(8,128)(2,1)S(1)} %bitcast.421, bf16[768,768]{1,0:T(8,128)(2,1)S(1)} %bitcast.423, bf16[768,768]{1,0:T(8,128)(2,1)S(1)} %bitcast.425, bf16[768,768]{1,0:T(8,128)(2,1)S(1)} %bitcast.419), kind=kOutput, calls=%fused_computation.40 | convolution fusion | flops 1242562560 | bytes 9830400 | tf_op jit(solution)/shard_map/dot_general | solution.py:29
  215.9 5.3 %multiply_reduce_fusion = (f32[12,256]{1,0:T(8,128)S(1)}, f32[12,256,512]{2,1,0:T(8,128)S(1)}) fusion(f32[12,256,512]{2,1,0:T(8,128)} %copy-done.3, f32[12,256]{1,0:T(8,128)S(1)} %log_add_fusion.1, bf16[256,12,64]{0,2,1:T(8,128)(2,1)} %bitcast.378, bf16[512,12,64]{0,2,1:T(8,128)(2,1)} %bitcast.390), kind=kOutput, calls=%fused_computation.9 | convolution fusion | flops 206042112 | bytes 13787136 | tf_op jit(solution)/shard_map/qhd,khd->hqk/dot_general | solution.py:74
  251.6 4.5 convolution_convert_fusion.7
  262.1 8.5 %sort.4 = (bf16[4,4,96,768]{3,2,1,0:T(8,128)(2,1)S(1)}, bf16[4,4,96,768]{3,2,1,0:T(8,128)(2,1)}) custom-call(s32[3]{0:T(128)S(1)} %pad_add_fusion.1.where, bf16[4,4,2,96,768]{4,3,2,1,0:T(8,128)(2,1)S(1)} %pad_maximum_fusion.2.blocks), custom_call_target="tpu_custom_call" | custom-call | bytes 9437184 | tf_op jit(solution)/shard_map/sort/pallas_call | solution.py:207
  293.5 7.0 %sort.5 = (bf16[4,4,96,768]{3,2,1,0:T(8,128)(2,1)S(1)}, bf16[4,4,96,768]{3,2,1,0:T(8,128)(2,1)S(1)}) custom-call(s32[3]{0:T(128)S(1)} %pad_add_fusion.1.where, bf16[4,4,2,96,768]{4,3,2,1,0:T(8,128)(2,1)S(1)} %pad_maximum_fusion.3.blocks), custom_call_target="tpu_custom_call" | custom-call | bytes 9437184 | tf_op jit(solution)/shard_map/sort/pallas_call | solution.py:207
  306.9 7.0 %sort.7 = (bf16[4,4,96,768]{3,2,1,0:T(8,128)(2,1)S(1)}, bf16[4,4,96,768]{3,2,1,0:T(8,128)(2,1)S(1)}) custom-call(s32[3]{0:T(128)S(1)} %pad_add_fusion.1.where, bf16[4,4,2,96,768]{4,3,2,1,0:T(8,128)(2,1)S(1)} %bitcast.346), custom_call_target="tpu_custom_call" | custom-call | bytes 9437184 | tf_op jit(solution)/shard_map/sort/pallas_call | solution.py:207
  317.5 4.0 collective-permute-done.68
  322.2 5.1 %collective-permute-done.69 = bf16[8,9504]{1,0:T(8,128)(2,1)S(1)} collective-permute-done((bf16[8,9504]{1,0:T(8,128)(2,1)S(1)}, bf16[8,9504]{1,0:T(8,128)(2,1)S(1)}, u32[]{:S(2)}, u32[]{:S(2)}) %collective-permute-start.69) | collective-permute-done | bytes 152096 | tf_op jit(solution)/shard_map/ppermute | solution.py:139
  334.2 7.0 %sort.6 = (bf16[4,4,96,768]{3,2,1,0:T(8,128)(2,1)S(1)}, bf16[4,4,96,768]{3,2,1,0:T(8,128)(2,1)S(1)}) custom-call(s32[3]{0:T(128)S(1)} %pad_add_fusion.1.where, bf16[4,4,2,96,768]{4,3,2,1,0:T(8,128)(2,1)S(1)} %pad_maximum_fusion.4.blocks), custom_call_target="tpu_custom_call" | custom-call | bytes 9437184 | tf_op jit(solution)/shard_map/sort/pallas_call | solution.py:207
  346.3 5.9 %fusion.73 = f32[128,9504]{0,1:T(8,128)} fusion(bf16[8,9504]{1,0:T(8,128)(2,1)S(1)} %collective-permute-done.69, bf16[8,9504]{1,0:T(8,128)(2,1)S(1)} %add_convert_fusion.8, f32[8,128]{1,0:T(8,128)S(1)} %copy-done.77), kind=kOutput, calls=%fused_computation.214 | convolution fusion | flops 117022464 | bytes 5174272 | tf_op jit(solution)/shard_map/dot_general | solution.py:414
  363.2 22.1 %collective-permute-done.33 = bf16[2,4,96,768]{3,2,1,0:T(8,128)(2,1)S(1)} collective-permute-done((bf16[2,4,96,768]{3,2,1,0:T(8,128)(2,1)S(1)}, bf16[2,4,96,768]{3,2,1,0:T(8,128)(2,1)S(1)}, u32[]{:S(2)}, u32[]{:S(2)}) %collective-permute-start.33) | collective-permute-done | bytes 1179680 | tf_op jit(solution)/shard_map/ppermute | solution.py:139
  388.7 23.5 %collective-permute-done.57 = bf16[2,4,96,768]{3,2,1,0:T(8,128)(2,1)S(1)} collective-permute-done((bf16[2,4,96,768]{3,2,1,0:T(8,128)(2,1)S(1)}, bf16[2,4,96,768]{3,2,1,0:T(8,128)(2,1)S(1)}, u32[]{:S(2)}, u32[]{:S(2)}) %collective-permute-start.57) | collective-permute-done | bytes 1179680 | tf_op jit(solution)/shard_map/ppermute | solution.py:135
  415.9 8.9 %collective-permute-done.34 = bf16[4,96,768]{2,1,0:T(8,128)(2,1)S(1)} collective-permute-done((bf16[4,96,768]{2,1,0:T(8,128)(2,1)S(1)}, bf16[4,96,768]{2,1,0:T(8,128)(2,1)S(1)}, u32[]{:S(2)}, u32[]{:S(2)}) %collective-permute-start.34) | collective-permute-done | bytes 589856 | tf_op jit(solution)/shard_map/ppermute | solution.py:135
  429.2 5.4 %collective-permute-done.58 = bf16[4,96,768]{2,1,0:T(8,128)(2,1)S(1)} collective-permute-done((bf16[4,96,768]{2,1,0:T(8,128)(2,1)S(1)}, bf16[4,96,768]{2,1,0:T(8,128)(2,1)S(1)}, u32[]{:S(2)}, u32[]{:S(2)}) %collective-permute-start.58) | collective-permute-done | bytes 589856 | tf_op jit(solution)/shard_map/ppermute | solution.py:139
  445.6 4.5 collective-permute-start.59
  450.1 3.9 collective-permute-start.53
  454.0 6.7 %collective-permute-done.43 = bf16[96,768]{1,0:T(8,128)(2,1)S(1)} collective-permute-done((bf16[96,768]{1,0:T(8,128)(2,1)S(1)}, bf16[96,768]{1,0:T(8,128)(2,1)S(1)}, u32[]{:S(2)}, u32[]{:S(2)}) %collective-permute-start.43) | collective-permute-done | bytes 147488 | tf_op jit(solution)/shard_map/ppermute | solution.py:147
  460.8 4.8 collective-permute-start.51
  467.1 5.2 %collective-permute-done.59 = bf16[96,768]{1,0:T(8,128)(2,1)S(1)} collective-permute-done((bf16[96,768]{1,0:T(8,128)(2,1)S(1)}, bf16[96,768]{1,0:T(8,128)(2,1)S(1)}, u32[]{:S(2)}, u32[]{:S(2)}) %collective-permute-start.59) | collective-permute-done | bytes 147488 | tf_op jit(solution)/shard_map/ppermute | solution.py:147
  483.2 5.0 collective-permute-done.39
  488.3 6.3 %collective-permute-done.47 = bf16[2,96,768]{2,1,0:T(8,128)(2,1)S(1)} collective-permute-done((bf16[2,96,768]{2,1,0:T(8,128)(2,1)S(1)}, bf16[2,96,768]{2,1,0:T(8,128)(2,1)S(1)}, u32[]{:S(2)}, u32[]{:S(2)}) %collective-permute-start.47) | collective-permute-done | bytes 294944 | tf_op jit(solution)/shard_map/ppermute | solution.py:139
  496.3 4.2 collective-permute-done.63
  (545 shorter events, 265.9 us)
Async XLA Ops:
  2.7 31.1 %collective-permute-start.10 = (bf16[96,768]{1,0:T(8,128)(2,1)S(1)}, bf16[96,768]{1,0:T(8,128)(2,1)}, u32[]{:S(2)}, u32[]{:S(2)}) collective-permute-start(bf16[96,768]{1,0:T(8,128)(2,1)S(1)} %bitcast.441), channel_id=1, source_target_pairs={{0,6},{1,7},{2,0},{3,1},{4,2},{5,3},{6,4},{7,5},{8,14},{9,15},{10,... | collective-permute-start | bytes 442376 | tf_op jit(solution)/shard_map/ppermute | solution.py:147
  7.8 26.4 %collective-permute-start.9 = (bf16[96,768]{1,0:T(8,128)(2,1)S(1)}, bf16[96,768]{1,0:T(8,128)(2,1)}, u32[]{:S(2)}, u32[]{:S(2)}) collective-permute-start(bf16[96,768]{1,0:T(8,128)(2,1)S(1)} %bitcast.442), channel_id=1, source_target_pairs={{0,4},{1,5},{2,6},{3,7},{4,0},{5,1},{6,2},{7,3},{8,12},{9,13},{10,... | collective-permute-start | bytes 442376 | tf_op jit(solution)/shard_map/ppermute | solution.py:147
  7.8 29.9 %collective-permute-start.8 = (bf16[96,768]{1,0:T(8,128)(2,1)S(1)}, bf16[96,768]{1,0:T(8,128)(2,1)}, u32[]{:S(2)}, u32[]{:S(2)}) collective-permute-start(bf16[96,768]{1,0:T(8,128)(2,1)S(1)} %bitcast.443), channel_id=1, source_target_pairs={{0,2},{1,3},{2,4},{3,5},{4,6},{5,7},{6,0},{7,1},{8,10},{9,11},{10,... | collective-permute-start | bytes 442376 | tf_op jit(solution)/shard_map/ppermute | solution.py:147
  10.9 35.0 %collective-permute-start.16 = (bf16[96,768]{1,0:T(8,128)(2,1)S(1)}, bf16[96,768]{1,0:T(8,128)(2,1)}, u32[]{:S(2)}, u32[]{:S(2)}) collective-permute-start(bf16[96,768]{1,0:T(8,128)(2,1)S(1)} %bitcast.438), channel_id=1, source_target_pairs={{0,6},{1,7},{2,0},{3,1},{4,2},{5,3},{6,4},{7,5},{8,14},{9,15},{10,... | collective-permute-start | bytes 442376 | tf_op jit(solution)/shard_map/ppermute | solution.py:147
  46.9 25.0 %collective-permute-start.11 = (bf16[4,96,768]{2,1,0:T(8,128)(2,1)S(1)}, bf16[4,96,768]{2,1,0:T(8,128)(2,1)S(1)}, u32[]{:S(2)}, u32[]{:S(2)}) collective-permute-start(bf16[4,96,768]{2,1,0:T(8,128)(2,1)S(1)} %get-tuple-element.112), channel_id=1, source_target_pairs={{0,8},{1,9},{2,10},{3,11},{4,12},{5,13},{6,14},{7,15},{8,0},{9,1},... | collective-permute-start | bytes 1769480 | tf_op jit(solution)/shard_map/ppermute | solution.py:135
  71.9 28.2 %collective-permute-start.29 = (bf16[4,96,768]{2,1,0:T(8,128)(2,1)S(1)}, bf16[4,96,768]{2,1,0:T(8,128)(2,1)S(1)}, u32[]{:S(2)}, u32[]{:S(2)}) collective-permute-start(bf16[4,96,768]{2,1,0:T(8,128)(2,1)S(1)} %get-tuple-element.104), channel_id=1, source_target_pairs={{0,16},{1,17},{2,18},{3,19},{4,20},{5,21},{6,22},{7,23},{8,24},{9,... | collective-permute-start | bytes 1769480 | tf_op jit(solution)/shard_map/ppermute | solution.py:139
  73.5 30.5 %collective-permute-start.23 = (bf16[4,96,768]{2,1,0:T(8,128)(2,1)S(1)}, bf16[4,96,768]{2,1,0:T(8,128)(2,1)S(1)}, u32[]{:S(2)}, u32[]{:S(2)}) collective-permute-start(bf16[4,96,768]{2,1,0:T(8,128)(2,1)S(1)} %get-tuple-element.98), channel_id=1, source_target_pairs={{0,8},{1,9},{2,10},{3,11},{4,12},{5,13},{6,14},{7,15},{8,0},{9,1},... | collective-permute-start | bytes 1769480 | tf_op jit(solution)/shard_map/ppermute | solution.py:135
  76.0 49.4 %collective-permute-start.12 = (bf16[2,4,96,768]{3,2,1,0:T(8,128)(2,1)S(1)}, bf16[2,4,96,768]{3,2,1,0:T(8,128)(2,1)S(1)}, u32[]{:S(2)}, u32[]{:S(2)}) collective-permute-start(bf16[2,4,96,768]{3,2,1,0:T(8,128)(2,1)S(1)} %pad_maximum_fusion.16), channel_id=1, source_target_pairs={{0,16},{1,17},{2,18},{3,19},{4,20},{5,21},{6,22},{7,23},{8,24},{9,... | collective-permute-start | bytes 3538952 | tf_op jit(solution)/shard_map/ppermute | solution.py:139
  89.0 51.7 %collective-permute-start.18 = (bf16[2,4,96,768]{3,2,1,0:T(8,128)(2,1)}, bf16[2,4,96,768]{3,2,1,0:T(8,128)(2,1)}, u32[]{:S(2)}, u32[]{:S(2)}) collective-permute-start(bf16[2,4,96,768]{3,2,1,0:T(8,128)(2,1)} %get-tuple-element.65), channel_id=1, source_target_pairs={{0,8},{1,9},{2,10},{3,11},{4,12},{5,13},{6,14},{7,15},{8,0},{9,1},... | collective-permute-start | bytes 3538952 | tf_op jit(solution)/shard_map/ppermute | solution.py:135
  101.6 42.6 %collective-permute-start.30 = (bf16[2,4,96,768]{3,2,1,0:T(8,128)(2,1)}, bf16[2,4,96,768]{3,2,1,0:T(8,128)(2,1)}, u32[]{:S(2)}, u32[]{:S(2)}) collective-permute-start(bf16[2,4,96,768]{3,2,1,0:T(8,128)(2,1)} %get-tuple-element.63), channel_id=1, source_target_pairs={{0,8},{1,9},{2,10},{3,11},{4,12},{5,13},{6,14},{7,15},{8,0},{9,1},... | collective-permute-start | bytes 3538952 | tf_op jit(solution)/shard_map/ppermute | solution.py:135
  106.0 41.8 %collective-permute-start.24 = (bf16[2,4,96,768]{3,2,1,0:T(8,128)(2,1)}, bf16[2,4,96,768]{3,2,1,0:T(8,128)(2,1)}, u32[]{:S(2)}, u32[]{:S(2)}) collective-permute-start(bf16[2,4,96,768]{3,2,1,0:T(8,128)(2,1)} %pad_maximum_fusion.18), channel_id=1, source_target_pairs={{0,16},{1,17},{2,18},{3,19},{4,20},{5,21},{6,22},{7,23},{8,24},{9,... | collective-permute-start | bytes 3538952 | tf_op jit(solution)/shard_map/ppermute | solution.py:139
  127.0 23.8 %collective-permute-start.13 = (bf16[4,4,96,768]{3,2,1,0:T(8,128)(2,1)}, bf16[4,4,96,768]{3,2,1,0:T(8,128)(2,1)}, u32[]{:S(2)}, u32[]{:S(2)}) collective-permute-start(bf16[4,4,96,768]{3,2,1,0:T(8,128)(2,1)} %pad_maximum_fusion.6.own), channel_id=1, source_target_pairs={{0,1},{1,0},{2,3},{3,2},{4,5},{5,4},{6,7},{7,6},{8,9},{9,8},{10,11... | collective-permute-start | bytes 7077896 | tf_op jit(solution)/shard_map/ppermute | solution.py:143
  144.1 20.1 %collective-permute-start.19 = (bf16[4,4,96,768]{3,2,1,0:T(8,128)(2,1)}, bf16[4,4,96,768]{3,2,1,0:T(8,128)(2,1)}, u32[]{:S(2)}, u32[]{:S(2)}) collective-permute-start(bf16[4,4,96,768]{3,2,1,0:T(8,128)(2,1)} %bitcast.41.own), channel_id=1, source_target_pairs={{0,1},{1,0},{2,3},{3,2},{4,5},{5,4},{6,7},{7,6},{8,9},{9,8},{10,11... | collective-permute-start | bytes 7077896 | tf_op jit(solution)/shard_map/ppermute | solution.py:143
  147.4 29.2 %collective-permute-start.31 = (bf16[4,4,96,768]{3,2,1,0:T(8,128)(2,1)}, bf16[4,4,96,768]{3,2,1,0:T(8,128)(2,1)}, u32[]{:S(2)}, u32[]{:S(2)}) collective-permute-start(bf16[4,4,96,768]{3,2,1,0:T(8,128)(2,1)} %bitcast.79.own), channel_id=1, source_target_pairs={{0,1},{1,0},{2,3},{3,2},{4,5},{5,4},{6,7},{7,6},{8,9},{9,8},{10,11... | collective-permute-start | bytes 7077896 | tf_op jit(solution)/shard_map/ppermute | solution.py:143
  150.6 37.1 %collective-permute-start.25 = (bf16[4,4,96,768]{3,2,1,0:T(8,128)(2,1)}, bf16[4,4,96,768]{3,2,1,0:T(8,128)(2,1)}, u32[]{:S(2)}, u32[]{:S(2)}) collective-permute-start(bf16[4,4,96,768]{3,2,1,0:T(8,128)(2,1)} %pad_maximum_fusion.9.own), channel_id=1, source_target_pairs={{0,1},{1,0},{2,3},{3,2},{4,5},{5,4},{6,7},{7,6},{8,9},{9,8},{10,11... | collective-permute-start | bytes 7077896 | tf_op jit(solution)/shard_map/ppermute | solution.py:143
  270.6 83.2 %collective-permute-start.32 = (bf16[4,4,96,768]{3,2,1,0:T(8,128)(2,1)}, bf16[4,4,96,768]{3,2,1,0:T(8,128)(2,1)}, u32[]{:S(2)}, u32[]{:S(2)}) collective-permute-start(bf16[4,4,96,768]{3,2,1,0:T(8,128)(2,1)} %get-tuple-element.22), channel_id=1, source_target_pairs={{0,1},{1,0},{2,3},{3,2},{4,5},{5,4},{6,7},{7,6},{8,9},{9,8},{10,11... | collective-permute-start | bytes 7077896 | tf_op jit(solution)/shard_map/ppermute | solution.py:143
  300.5 56.6 %collective-permute-start.40 = (bf16[4,4,96,768]{3,2,1,0:T(8,128)(2,1)S(1)}, bf16[4,4,96,768]{3,2,1,0:T(8,128)(2,1)S(1)}, u32[]{:S(2)}, u32[]{:S(2)}) collective-permute-start(bf16[4,4,96,768]{3,2,1,0:T(8,128)(2,1)S(1)} %get-tuple-element.24), channel_id=1, source_target_pairs={{0,1},{1,0},{2,3},{3,2},{4,5},{5,4},{6,7},{7,6},{8,9},{9,8},{10,11... | collective-permute-start | bytes 7077896 | tf_op jit(solution)/shard_map/ppermute | solution.py:143
  313.9 45.6 %collective-permute-start.56 = (bf16[4,4,96,768]{3,2,1,0:T(8,128)(2,1)S(1)}, bf16[4,4,96,768]{3,2,1,0:T(8,128)(2,1)S(1)}, u32[]{:S(2)}, u32[]{:S(2)}) collective-permute-start(bf16[4,4,96,768]{3,2,1,0:T(8,128)(2,1)S(1)} %get-tuple-element.28), channel_id=1, source_target_pairs={{0,1},{1,0},{2,3},{3,2},{4,5},{5,4},{6,7},{7,6},{8,9},{9,8},{10,11... | collective-permute-start | bytes 7077896 | tf_op jit(solution)/shard_map/ppermute | solution.py:143
  356.4 28.9 %collective-permute-start.33 = (bf16[2,4,96,768]{3,2,1,0:T(8,128)(2,1)S(1)}, bf16[2,4,96,768]{3,2,1,0:T(8,128)(2,1)S(1)}, u32[]{:S(2)}, u32[]{:S(2)}) collective-permute-start(bf16[2,4,96,768]{3,2,1,0:T(8,128)(2,1)S(1)} %slice.353), channel_id=1, source_target_pairs={{0,16},{1,17},{2,18},{3,19},{4,20},{5,21},{6,22},{7,23},{8,24},{9,... | collective-permute-start | bytes 3538952 | tf_op jit(solution)/shard_map/ppermute | solution.py:139
  357.9 29.4 %collective-permute-start.41 = (bf16[2,4,96,768]{3,2,1,0:T(8,128)(2,1)S(1)}, bf16[2,4,96,768]{3,2,1,0:T(8,128)(2,1)S(1)}, u32[]{:S(2)}, u32[]{:S(2)}) collective-permute-start(bf16[2,4,96,768]{3,2,1,0:T(8,128)(2,1)S(1)} %slice.304), channel_id=1, source_target_pairs={{0,8},{1,9},{2,10},{3,11},{4,12},{5,13},{6,14},{7,15},{8,0},{9,1},... | collective-permute-start | bytes 3538952 | tf_op jit(solution)/shard_map/ppermute | solution.py:135
  360.3 51.8 %collective-permute-start.57 = (bf16[2,4,96,768]{3,2,1,0:T(8,128)(2,1)S(1)}, bf16[2,4,96,768]{3,2,1,0:T(8,128)(2,1)S(1)}, u32[]{:S(2)}, u32[]{:S(2)}) collective-permute-start(bf16[2,4,96,768]{3,2,1,0:T(8,128)(2,1)S(1)} %slice.324), channel_id=1, source_target_pairs={{0,8},{1,9},{2,10},{3,11},{4,12},{5,13},{6,14},{7,15},{8,0},{9,1},... | collective-permute-start | bytes 3538952 | tf_op jit(solution)/shard_map/ppermute | solution.py:135
  361.8 52.2 %collective-permute-start.49 = (bf16[2,4,96,768]{3,2,1,0:T(8,128)(2,1)S(1)}, bf16[2,4,96,768]{3,2,1,0:T(8,128)(2,1)S(1)}, u32[]{:S(2)}, u32[]{:S(2)}) collective-permute-start(bf16[2,4,96,768]{3,2,1,0:T(8,128)(2,1)S(1)} %slice.373), channel_id=1, source_target_pairs={{0,16},{1,17},{2,18},{3,19},{4,20},{5,21},{6,22},{7,23},{8,24},{9,... | collective-permute-start | bytes 3538952 | tf_op jit(solution)/shard_map/ppermute | solution.py:139
  385.6 39.1 %collective-permute-start.34 = (bf16[4,96,768]{2,1,0:T(8,128)(2,1)S(1)}, bf16[4,96,768]{2,1,0:T(8,128)(2,1)S(1)}, u32[]{:S(2)}, u32[]{:S(2)}) collective-permute-start(bf16[4,96,768]{2,1,0:T(8,128)(2,1)S(1)} %slice_bitcast_fusion.6), channel_id=1, source_target_pairs={{0,8},{1,9},{2,10},{3,11},{4,12},{5,13},{6,14},{7,15},{8,0},{9,1},... | collective-permute-start | bytes 1769480 | tf_op jit(solution)/shard_map/ppermute | solution.py:135
  387.6 39.9 %collective-permute-start.42 = (bf16[4,96,768]{2,1,0:T(8,128)(2,1)S(1)}, bf16[4,96,768]{2,1,0:T(8,128)(2,1)S(1)}, u32[]{:S(2)}, u32[]{:S(2)}) collective-permute-start(bf16[4,96,768]{2,1,0:T(8,128)(2,1)S(1)} %slice_bitcast_fusion.4), channel_id=1, source_target_pairs={{0,16},{1,17},{2,18},{3,19},{4,20},{5,21},{6,22},{7,23},{8,24},{9,... | collective-permute-start | bytes 1769480 | tf_op jit(solution)/shard_map/ppermute | solution.py:139
  412.5 22.1 %collective-permute-start.58 = (bf16[4,96,768]{2,1,0:T(8,128)(2,1)S(1)}, bf16[4,96,768]{2,1,0:T(8,128)(2,1)S(1)}, u32[]{:S(2)}, u32[]{:S(2)}) collective-permute-start(bf16[4,96,768]{2,1,0:T(8,128)(2,1)S(1)} %slice_bitcast_fusion), channel_id=1, source_target_pairs={{0,16},{1,17},{2,18},{3,19},{4,20},{5,21},{6,22},{7,23},{8,24},{9,... | collective-permute-start | bytes 1769480 | tf_op jit(solution)/shard_map/ppermute | solution.py:139
  414.3 22.7 %collective-permute-start.50 = (bf16[4,96,768]{2,1,0:T(8,128)(2,1)S(1)}, bf16[4,96,768]{2,1,0:T(8,128)(2,1)S(1)}, u32[]{:S(2)}, u32[]{:S(2)}) collective-permute-start(bf16[4,96,768]{2,1,0:T(8,128)(2,1)S(1)} %slice_bitcast_fusion.2), channel_id=1, source_target_pairs={{0,8},{1,9},{2,10},{3,11},{4,12},{5,13},{6,14},{7,15},{8,0},{9,1},... | collective-permute-start | bytes 1769480 | tf_op jit(solution)/shard_map/ppermute | solution.py:135
  437.6 23.1 %collective-permute-start.43 = (bf16[96,768]{1,0:T(8,128)(2,1)S(1)}, bf16[96,768]{1,0:T(8,128)(2,1)S(1)}, u32[]{:S(2)}, u32[]{:S(2)}) collective-permute-start(bf16[96,768]{1,0:T(8,128)(2,1)S(1)} %get-tuple-element.87), channel_id=1, source_target_pairs={{0,4},{1,5},{2,6},{3,7},{4,0},{5,1},{6,2},{7,3},{8,12},{9,13},{10,... | collective-permute-start | bytes 442376 | tf_op jit(solution)/shard_map/ppermute | solution.py:147
  439.1 21.6 %collective-permute-start.61 = (bf16[96,768]{1,0:T(8,128)(2,1)S(1)}, bf16[96,768]{1,0:T(8,128)(2,1)S(1)}, u32[]{:S(2)}, u32[]{:S(2)}) collective-permute-start(bf16[96,768]{1,0:T(8,128)(2,1)S(1)} %get-tuple-element.74), channel_id=1, source_target_pairs={{0,6},{1,7},{2,0},{3,1},{4,2},{5,3},{6,4},{7,5},{8,14},{9,15},{10,... | collective-permute-start | bytes 442376 | tf_op jit(solution)/shard_map/ppermute | solution.py:147
  441.4 24.1 %collective-permute-start.60 = (bf16[96,768]{1,0:T(8,128)(2,1)S(1)}, bf16[96,768]{1,0:T(8,128)(2,1)S(1)}, u32[]{:S(2)}, u32[]{:S(2)}) collective-permute-start(bf16[96,768]{1,0:T(8,128)(2,1)S(1)} %get-tuple-element.75), channel_id=1, source_target_pairs={{0,2},{1,3},{2,4},{3,5},{4,6},{5,7},{6,0},{7,1},{8,10},{9,11},{10,... | collective-permute-start | bytes 442376 | tf_op jit(solution)/shard_map/ppermute | solution.py:147
  445.6 26.7 %collective-permute-start.59 = (bf16[96,768]{1,0:T(8,128)(2,1)S(1)}, bf16[96,768]{1,0:T(8,128)(2,1)S(1)}, u32[]{:S(2)}, u32[]{:S(2)}) collective-permute-start(bf16[96,768]{1,0:T(8,128)(2,1)S(1)} %get-tuple-element.73), channel_id=1, source_target_pairs={{0,4},{1,5},{2,6},{3,7},{4,0},{5,1},{6,2},{7,3},{8,12},{9,13},{10,... | collective-permute-start | bytes 442376 | tf_op jit(solution)/shard_map/ppermute | solution.py:147
  450.1 23.8 %collective-permute-start.53 = (bf16[96,768]{1,0:T(8,128)(2,1)S(1)}, bf16[96,768]{1,0:T(8,128)(2,1)S(1)}, u32[]{:S(2)}, u32[]{:S(2)}) collective-permute-start(bf16[96,768]{1,0:T(8,128)(2,1)S(1)} %get-tuple-element.81), channel_id=1, source_target_pairs={{0,6},{1,7},{2,0},{3,1},{4,2},{5,3},{6,4},{7,5},{8,14},{9,15},{10,... | collective-permute-start | bytes 442376 | tf_op jit(solution)/shard_map/ppermute | solution.py:147
  482.2 21.4 %collective-permute-start.55 = (bf16[2,96,768]{2,1,0:T(8,128)(2,1)S(1)}, bf16[2,96,768]{2,1,0:T(8,128)(2,1)S(1)}, u32[]{:S(2)}, u32[]{:S(2)}) collective-permute-start(bf16[2,96,768]{2,1,0:T(8,128)(2,1)S(1)} %pad_maximum_fusion.41), channel_id=1, source_target_pairs={{0,16},{1,17},{2,18},{3,19},{4,20},{5,21},{6,22},{7,23},{8,24},{9,... | collective-permute-start | bytes 884744 | tf_op jit(solution)/shard_map/ppermute | solution.py:139
  (151 other events, 1571.3 us)
